TPU v7x, 32 devices: a whole 2x2x4 slice. The times are simulated.
32 devices in a mesh: rep: 4 (over y, core), shard: 4 (over z), tp: 2 (over x).
Axes of the slice: x: 2, y: 2, z: 4, core: 2. Of those that a mesh axis runs over, the one named last changes fastest.
Arguments:
- hidden_in: bfloat16 [8192, 8192], P(('rep', 'shard', 'tp')), may hold values from -6 to 6
- lengths: int32 [16], P(('rep', 'shard')), may hold values from 128 to 512, as said below
- kv_grad_out: bfloat16 [8192, 2, 1024], P(('rep', 'shard'), None, 'tp'), may hold values from -384 to 384
- master: float32 [8192, 2, 1024], P('shard', None, 'tp'), may hold values from -0.0625 to 0.0625
- moment_one: float32 [8192, 2, 1024], P('shard', None, 'tp'), may hold values from -3 to 3
- moment_two: float32 [8192, 2, 1024], P('shard', None, 'tp'), may hold values from 0.05 to 2
Outputs:
- new_master: float32 [8192, 2, 1024], P('shard', None, 'tp')
- new_moment_one: float32 [8192, 2, 1024], P('shard', None, 'tp')
- new_moment_two: float32 [8192, 2, 1024], P('shard', None, 'tp')
- fresh_kv: bfloat16 [8192, 2, 1024], P(('rep', 'shard'), None, 'tp')
Inputs may be any that keep to these rules, and one draw needn't show every extreme that they name: In block b only its first lengths[b] tokens are valid.
All inputs are finite; a program needn't handle non-finite values.
Results may differ from a plain program's by a relative error of at most 0.014.
Values may be sent and summed in bfloat16 or wider, within the bound.
No kernel may reach another device: no remote copies, remote signals or barrier semaphores. Data moves between devices by JAX's collectives and lax.ppermute only.
A program may use at most 192 MiB of HBM per device.

v0:
```python
import functools

import jax
import jax.numpy as jnp
from jax import lax
from jax.experimental import pallas as pl
from jax.experimental.pallas import tpu as pltpu
from jax.sharding import PartitionSpec as P

beta_one = 0.9
beta_two = 0.95
step_count = 20
rate = 0.002
decay = 0.1
epsilon = 1e-08

LANES = 128
GROUPS = 4
LOADS = 2
VMEM_BYTES = 56 * 1024 * 1024

SMEM = pl.BlockSpec(memory_space=pltpu.SMEM)


def adamw(master, moment_one, moment_two, grad):
    first = beta_one * moment_one + (1.0 - beta_one) * grad
    second = beta_two * moment_two + (1.0 - beta_two) * grad * grad
    first_hat = first / (1.0 - beta_one**step_count)
    second_hat = second / (1.0 - beta_two**step_count)
    updated = master - rate * (first_hat / (jnp.sqrt(second_hat) + epsilon) + decay * master)
    return (updated, first, second)


def lane_rows(array):
    rows, two, features = array.shape
    split = array.reshape(rows, two, features // LANES, LANES)
    return split.transpose(0, 2, 1, 3).reshape(rows * two * features // LANES, LANES)


def from_lane_rows(array, rows, features):
    split = array.reshape(rows, features // LANES, 2, LANES)
    return split.transpose(0, 2, 1, 3).reshape(rows, 2, features)


def slots(features):
    return [half * features + tile * LANES for tile in range(features // LANES) for half in range(2)]


def call(kernel, out_shape, flops, moved, **kwargs):
    return pl.pallas_call(
        kernel,
        out_shape=out_shape,
        cost_estimate=pl.CostEstimate(flops=flops, bytes_accessed=moved, transcendentals=0),
        compiler_params=pltpu.CompilerParams(vmem_limit_bytes=VMEM_BYTES),
        **kwargs,
    )


def full(shape):
    return pl.BlockSpec(shape, lambda *_: (0,) * len(shape))


def f32(ref):
    return ref[...].astype(jnp.float32)


def pack(hidden, rep, loads, replicas, rows):
    tokens = hidden.shape[0]
    specs, shapes, orders = [], [], []
    for load in loads:
        for k in range(replicas):
            at = len(orders)
            for start, part, order in load:
                for _ in order:
                    at += 1

                    def index(i, place, at=at, k=k, start=start, part=part):
                        return (0, (place[at] * replicas + (place[0] ^ k)) * (rows // part) + start // part)

                    specs.append(pl.BlockSpec((tokens, part), index))
            shapes.append((sum(part * len(order) for _, part, order in load), tokens))
        orders += [shard for _, _, order in load for shard in order]

    def kernel(place, *refs):
        sources, outs = iter(refs[: len(specs)]), iter(refs[len(specs) :])
        for load in loads:
            for k in range(replicas):
                out, row = next(outs), 0
                for _, part, order in load:
                    for _ in order:
                        out[row : row + part, :] = next(sources)[...].T
                        row += part

    outs = call(
        kernel,
        [jax.ShapeDtypeStruct(shape, hidden.dtype) for shape in shapes],
        0,
        4 * sum(shape[0] * shape[1] for shape in shapes),
        grid_spec=pltpu.PrefetchScalarGridSpec(
            num_scalar_prefetch=1,
            grid=(1,),
            in_specs=specs,
            out_specs=[full(shape) for shape in shapes],
        ),
    )(jnp.stack([rep, *orders]), *[hidden] * len(specs))
    return [outs[i : i + replicas] for i in range(0, len(outs), replicas)]


def mask(cotan, place, pairs):
    block, _, features = cotan.shape
    width, tokens = 2 * features, block // pairs
    per = width // LANES

    def kernel(place, source, out, count, scratch):
        scratch[...] = source[...].astype(jnp.float32)
        count[...] = jnp.full(count.shape, place[0]).astype(jnp.float32)
        for o in range(pairs):
            start = (place[1] ^ o) * tokens
            row = lax.broadcasted_iota(jnp.int32, (tokens, LANES), 0) + start
            for slot, column in enumerate(slots(features)):
                rows = scratch[pl.ds(start * per + slot, tokens, stride=per), :]
                out[o * tokens : (o + 1) * tokens, column : column + LANES] = jnp.where(
                    row < place[0], rows, 0.0
                ).astype(out.dtype)

    return call(
        kernel,
        [jax.ShapeDtypeStruct((block, width), cotan.dtype), jax.ShapeDtypeStruct((8, LANES), jnp.float32)],
        0,
        4 * block * width,
        grid=(1,),
        in_specs=[SMEM, full((block * per, LANES))],
        out_specs=[full((block, width)), full((8, LANES))],
        scratch_shapes=[pltpu.VMEM((block * per, LANES), jnp.float32)],
    )(place, lane_rows(cotan))


def fresh_weights(place, count, shares, params):
    part, width = shares[0][1].block_shape
    per = width // LANES

    def kernel(place, count, *refs):
        sources = refs[: len(shares)]
        master, first, second, weights, grad, scratch = refs[len(shares) :]
        grad[...] = sum(f32(source) for source in sources).astype(grad.dtype)
        scale = 1.0 / count[0:1, 0:1]
        starts = slots(width // 2)
        for slot, start in enumerate(starts):
            scratch[pl.ds(slot, part, stride=per), :] = grad[:, start : start + LANES].astype(jnp.float32)
        updated, _, _ = adamw(master[...], first[...], second[...], scratch[...] * scale)
        scratch[...] = updated
        for slot, start in enumerate(starts):
            weights[:, start : start + LANES] = scratch[pl.ds(slot, part, stride=per), :].astype(weights.dtype)

    param_spec = pl.BlockSpec((part * per, LANES), lambda i, place: (place[0], 0))
    return call(
        kernel,
        [jax.ShapeDtypeStruct((part, width), jnp.bfloat16)] * 2,
        20 * part * width,
        20 * part * width,
        grid_spec=pltpu.PrefetchScalarGridSpec(
            num_scalar_prefetch=1,
            grid=(1,),
            in_specs=[full((8, LANES)), *[spec for _, spec in shares], param_spec, param_spec, param_spec],
            out_specs=[pl.BlockSpec((part, width), lambda i, place: (0, 0))] * 2,
            scratch_shapes=[pltpu.VMEM((part * per, LANES), jnp.float32)],
        ),
    )(place, count, *[a for a, _ in shares], *params)


def update(me, count, grads, params, ks, block, before):
    rows, width = grads[0].shape
    per = width // LANES
    steps = rows // block
    first_k = min(ks)

    def kernel(place, count, *refs):
        sources = refs[: len(grads)]
        master, first, second = refs[len(grads) : len(grads) + 3]
        new_master, new_first, new_second, scratch = refs[-4:]
        scale = 1.0 / count[0:1, 0:1]
        for j, grad in enumerate(sources):

            @pl.when(pl.program_id(0) == j)
            def _(grad=grad):
                for slot, start in enumerate(slots(width // 2)):
                    scratch[pl.ds(slot, block, stride=per), :] = grad[:, start : start + LANES].astype(jnp.float32)

        updated, one, two = adamw(master[...], first[...], second[...], scratch[...] * scale)
        new_master[...] = updated
        new_first[...] = one
        new_second[...] = two

    def grad_spec(j):
        return pl.BlockSpec(
            (block, width), lambda k, i, me: (jnp.where(k == j, i, jnp.where(k < j, 0, steps - 1)), 0)
        )

    param_spec = pl.BlockSpec((block * per, LANES), lambda k, i, me: ((me[0] ^ (k + first_k)) * steps + i, 0))
    size = len(ks) * rows * width
    return call(
        kernel,
        [jax.ShapeDtypeStruct(params[0].shape, jnp.float32)] * 3,
        20 * size,
        26 * size,
        grid_spec=pltpu.PrefetchScalarGridSpec(
            num_scalar_prefetch=1,
            grid=(len(ks), steps),
            in_specs=[full((8, LANES))]
            + [grad_spec(j) for j in range(len(grads))]
            + [param_spec] * 3
            + [pl.BlockSpec(memory_space=pl.ANY)] * len(before),
            out_specs=[param_spec] * 3,
            scratch_shapes=[pltpu.VMEM((block * per, LANES), jnp.float32)],
        ),
        input_output_aliases={2 + len(grads) + 3 + i: i for i in range(len(before))},
    )(me, count, *grads, *params, *before)


def combine(shares, pair, pairs, rows):
    features = shares[0][0].shape[1]
    tokens, per = rows // pairs, 2 * features // LANES
    each = len(shares[0])

    def kernel(pair, *refs):
        out, scratch = refs[-2], refs[-1]
        for o in range(pairs):
            start = (pair[0] ^ o) * tokens
            for slot, column in enumerate(slots(features)):
                half, at = divmod(column, features)
                total = sum(
                    source[o * tokens : (o + 1) * tokens, at : at + LANES].astype(jnp.float32)
                    for source in refs[half * each : (half + 1) * each]
                )
                scratch[pl.ds(start * per + slot, tokens, stride=per), :] = total
        out[...] = scratch[...].astype(out.dtype)

    out = call(
        kernel,
        jax.ShapeDtypeStruct((rows * per, LANES), jnp.bfloat16),
        0,
        16 * rows * features,
        grid=(1,),
        in_specs=[SMEM] + [full((rows, features))] * (2 * each),
        out_specs=full((rows * per, LANES)),
        scratch_shapes=[pltpu.VMEM((rows * per, LANES), jnp.float32)],
    )(pair, *shares[0], *shares[1])
    return from_lane_rows(out, rows, features)


def after(value, *deps):
    return lax.optimization_barrier((value, *deps))[0] if deps else value


def swap(value, axis, k):
    if k == 0:
        return value
    return lax.ppermute(value, axis, [(i, i ^ k) for i in range(lax.axis_size(axis))])


def add(a, b):
    return (a.astype(jnp.float32) + b.astype(jnp.float32)).astype(jnp.bfloat16)


class Line:
    ends_to_inner = [(0, 1), (3, 2)]
    across = [(1, 2), (2, 1)]
    inner_to_ends = [(1, 0), (2, 3)]

    away_first = True

    def __init__(self, shard):
        self.end = (shard == 0) | (shard == 3)
        low = shard < 2
        self.order = [jnp.where(low, 3, 0), jnp.where(low, 2, 1), shard ^ 1, shard]

    def send(self, away, soon):
        return add(away, after(lax.ppermute(away, "shard", self.ends_to_inner), *soon))

    def settle(self, far, last, soon):
        part = last.shape[0] // 2
        got = lax.ppermute(far, "shard", self.across)
        near = add(last[:part], after(got, *soon)[:part])
        return [(last, 1), (got, 1), (swap(near, "shard", 1), 0)], near

    def gather(self, own, *waits):
        side = after(jnp.concatenate([swap(own, "shard", 1), own], axis=0), *waits)
        got = lax.ppermute(side, "shard", self.across)
        far = lax.ppermute(got, "shard", self.inner_to_ends)
        return [jnp.where(self.end, far, got), side]


class Halves:
    away_first = False

    def __init__(self, shard, shards):
        order, k = [0], shards // 2
        while k:
            order, k = [i + k for i in order] + order, k // 2
        self.shards = shards
        self.order = [shard ^ q for q in order[shards // 2 :] + order[: shards // 2]]

    def send(self, away, soon):
        return after(swap(away, "shard", 1), *soon)

    def settle(self, far, last, soon):
        shares, half, k, sent = [last, far], last.shape[0], 2, far
        while k < self.shards:
            sent = sum(v[v.shape[0] - half : v.shape[0] - half // 2].astype(jnp.float32) for v in shares)
            sent, half, k = sent.astype(jnp.bfloat16), half // 2, 2 * k
            shares.append(swap(sent, "shard", k // 2))
        return [(v, v.shape[0] // half - 1) for v in shares], sent

    def gather(self, own, *waits):
        blocks, k = own, self.shards // 2
        while k > 1:
            blocks, k = jnp.concatenate([swap(blocks, "shard", k), blocks], axis=0), k // 2
        return [swap(blocks, "shard", 1), blocks]


def local(hidden_in, lengths, kv_grad_out, master, moment_one, moment_two):
    replicas, shards, pairs = (lax.axis_size(name) for name in ("rep", "shard", "tp"))
    rep, shard, pair = (lax.axis_index(name).astype(jnp.int32) for name in ("rep", "shard", "tp"))
    tokens, depth = hidden_in.shape
    block, _, features = kv_grad_out.shape
    width = 2 * features
    rows = depth // (shards * replicas)
    near = replicas // 2
    parities = [k for k in range(replicas) if k % 2] + [k for k in range(replicas) if not k % 2]
    odd = replicas // 2 * block

    number = max(1, min(GROUPS, rows // LANES))
    part = rows // number
    ways = [Line(shard) if shards == 4 and g < number - 1 else Halves(shard, shards) for g in range(number)]
    groups = [(g * part, part, way.order) for g, way in enumerate(ways)]
    each = max(1, number // LOADS)
    loads = [groups[g : g + each] for g in range(0, number, each)]
    by_rows = (((0,), (0,)), ((), ()))

    count, k = jnp.full((8, LANES), lengths[0]).astype(jnp.float32), near
    count = count + swap(count, "rep", k)
    early, k = count, k // 2
    while k:
        count, k = count + swap(count, "rep", k), k // 2
    k = 1
    while k < shards:
        count, k = count + swap(count, "shard", k), 2 * k
    pieces = pack(hidden_in, rep, loads[:1], replicas, rows)
    cotan, _ = mask(kv_grad_out, jnp.stack([lengths[0], pair]), pairs)
    if len(loads) > 1:
        pieces += pack(hidden_in, after(rep, count), loads[1:], replicas, rows)
    arrived, sides, line = [], [], []

    def travel(n, *waits):
        arrived.append(
            [pieces[n][0]]
            + [swap(after(h, *waits) if k >= near else h, "rep", k) for k, h in enumerate(pieces[n]) if k]
        )
        sides.append([])

    def pair_up(n, ks, *waits):
        for k in ks:
            sent = after(arrived[n][k], *line[-2:-1], *waits)
            sides[n].append([arrived[n][k]] + [swap(sent, "tp", o) for o in range(1, pairs)])
            line.append(sides[n][-1][-1])

    def lay(n):
        return jnp.concatenate([p for k in parities for p in sides[n][k]], axis=1)

    low, high = range(near), range(near, replicas)
    travel(0, early)
    pair_up(0, low)
    pair_up(0, high, cotan)
    ready = [*arrived[0][near:], *line[:near], *(pieces[1] if len(loads) > 1 else [])]
    cotans = {0: cotan, near: swap(after(cotan, *ready), "rep", near)}
    for n in range(1, len(loads)):
        travel(n, *([cotans[near]] if n == 1 else arrived[n - 1][near:]))
        if n == 1:
            pair_up(1, low)
    k = near // 2
    while k:
        for have in list(cotans):
            cotans[have ^ k] = swap(cotans[have], "rep", k)
        k //= 2
    cotans = jnp.concatenate([cotans[k] for k in parities], axis=0)

    params = [lane_rows(a) for a in (master, moment_one, moment_two)]
    steps, summed, grads, fresh, gathered, places, inputs, last = [], [], [], [], [], [], [], None

    def project(rows, weights):
        return lax.dot_general(rows, weights, by_rows, preferred_element_type=jnp.float32)

    half = shards // 2 * part
    for n, load in enumerate(loads):
        laid = lay(n)
        if n:
            laid = after(laid, fresh[(n - 1) * each], *steps)
        for inside in range(len(load)):
            g, way = n * each + inside, ways[n * each + inside]
            if last is not None:
                laid = after(laid, last)
            if n + 1 < len(loads) and inside == 1:
                laid = after(laid, line[(n + 1) * replicas])
            row = inside * 2 * half
            far_row, near_row = (row, row + half) if way.away_first else (row + half, row)
            places.append((far_row, near_row))
            away = jnp.dot(laid[far_row : far_row + half], cotans, preferred_element_type=jnp.float32)
            away = away.astype(jnp.bfloat16)
            laid = after(laid, away)
            last = jnp.dot(laid[near_row : near_row + half], cotans, preferred_element_type=jnp.float32)
            last = last.astype(jnp.bfloat16)
            soon, then = [], []
            if not n and inside:
                away = after(away, far)
            if n + 1 < len(loads) and inside:
                soon = arrived[n + 1][near:]
            if n and inside:
                soon = [summed[each - 1][-1][0]]
            far = way.send(away, soon)
            if n + 1 < len(loads):
                pair_up(n + 1, range(near + inside, near + inside + 1 if inside < each - 1 else replicas), far)
                then = line[-1:]
            shares, passed = way.settle(far, last, then)
            steps.append(passed)
            summed.append(shares)
        for inside in range(len(load)):
            g = n * each + inside
            shares = summed[g]
            if n and inside == 0:
                shares = [(after(shares[0][0], steps[-1], *fresh[each - 1 : each]), shares[0][1])] + shares[1:]
            if not n and inside:
                shares = [(after(shares[0][0], gathered[0][0]), shares[0][1])] + shares[1:]
            if n and inside:
                shares = [(after(shares[0][0], fresh[each - 1], steps[each]), shares[0][1])] + shares[1:]
            place = (rep * number + g)[None]
            specs = [
                (v, pl.BlockSpec((part, width), lambda i, place, row=row: (row, 0))) for v, row in shares
            ]
            weights, grad = fresh_weights(place, count, specs, params)
            fresh.append(weights)
            grads.append(grad)
            if n + 1 == len(loads) or inside == 0:
                gathered.append(ways[g].gather(weights))
            if n and inside == 0:
                gathered.insert(1, ways[1].gather(fresh[1], steps[2]))
        inputs.append(laid)

    every = {0: jnp.concatenate(grads, axis=0)}
    k = near
    while k:
        for have in list(every):
            every[have ^ k] = swap(every[have], "rep", k)
        k //= 2

    total = None
    if len(loads) > 1:
        total = project(inputs[0], jnp.concatenate([w for g in range(each) for w in gathered[g]], axis=0))
    held = range(number - each, number)
    begin = min(places[g][1] for g in held)
    assert all(places[g][1] == begin + i * half for i, g in enumerate(held))
    product = project(
        inputs[-1][begin : begin + each * half], jnp.concatenate([gathered[g][1] for g in held], axis=0)
    )
    total = product if total is None else total + product
    here = after(inputs[-1], every[near], total)
    sums, turn = [], here
    for side in (slice(0, features), slice(features, width)):
        here = after(here, turn)
        ends = []
        for columns in (slice(0, odd), slice(odd, 2 * odd)):
            end = total[columns, side]
            for g in held:
                row = places[g][0]
                end = end + project(here[row : row + half, columns], gathered[g][0][:, side])
            ends.append(end.astype(jnp.bfloat16))
            here = after(here, ends[0])
        away, stay = ends
        shares, turn = [stay, swap(away, "rep", 1)], stay
        size, k = odd // 2, 2
        while k < replicas:
            sent = sum(v[size : 2 * size].astype(jnp.float32) for v in shares).astype(jnp.bfloat16)
            shares.append(swap(sent, "rep", k))
            size, k = size // 2, 2 * k
        sums.append(shares)
    fresh = combine(sums, pair[None], pairs, block)

    everyone = [after(every[0], sent)] + [every[k] for k in range(1, replicas)]
    updated = update(rep[None], count, everyone, params, range(replicas), min(rows, 256), [])
    updated = [from_lane_rows(a, master.shape[0], features) for a in updated]
    return (*updated, fresh)


def solution(mesh):
    in_specs = (
        P(("rep", "shard", "tp"), None),
        P(("rep", "shard")),
        P(("rep", "shard"), None, "tp"),
        P("shard", None, "tp"),
        P("shard", None, "tp"),
        P("shard", None, "tp"),
    )
    out_specs = (
        P("shard", None, "tp"),
        P("shard", None, "tp"),
        P("shard", None, "tp"),
        P(("rep", "shard"), None, "tp"),
    )
    return jax.shard_map(local, mesh=mesh, in_specs=in_specs, out_specs=out_specs, check_vma=False)
```

profile of v0, /device:TPU:0, one launch (start us, length us, event | category | flops | bytes accessed | tf_op | source)
XLA Modules:
  0.0 266.2 jit_solution(13423261568521789640)
XLA Ops:
  1.3 3.8 %shard_map.93 = (bf16[1024,256]{1,0:T(8,128)(2,1)}, bf16[1024,256]{1,0:T(8,128)(2,1)}, bf16[1024,256]{1,0:T(8,128)(2,1)}, bf16[1024,256]{1,0:T(8,128)(2,1)}) custom-call(s32[9]{0:T(128)} %stack.48.place, bf16[256,8192]{1,0:T(8,128)(2,1)} %refs_31_.3, bf16[256,8192]{1,0:T(8,128)(2,1)} %refs_31_.3, bf16[256,8192]{1,0:T(8,128)(2,1)} %refs_31_.3, ...), custom_call_target="tpu_custom_call" | custom-call | bytes 4194304 | tf_op jit(solution)/shard_map/pallas_call | solution.py:94
  6.3 2.6 collective-permute-start
  18.8 2.6 collective-permute-start.3
  22.0 3.2 %shard_map.94 = (bf16[512,1024]{1,0:T(8,128)(2,1)}, f32[8,128]{1,0:T(8,128)}) custom-call(s32[2]{0:T(128)} %pad_add_fusion.place, bf16[4096,128]{1,0:T(8,128)(2,1)} %bitcast.80), custom_call_target="tpu_custom_call" | custom-call | bytes 2097152 | tf_op jit(solution)/shard_map/pallas_call | solution.py:126
  26.5 3.9 %shard_map.95 = (bf16[1024,256]{1,0:T(8,128)(2,1)}, bf16[1024,256]{1,0:T(8,128)(2,1)}, bf16[1024,256]{1,0:T(8,128)(2,1)}, bf16[1024,256]{1,0:T(8,128)(2,1)}) custom-call(s32[9]{0:T(128)} %stack.54.place, bf16[256,8192]{1,0:T(8,128)(2,1)} %refs_31_.3, bf16[256,8192]{1,0:T(8,128)(2,1)} %refs_31_.3, bf16[256,8192]{1,0:T(8,128)(2,1)} %refs_31_.3, ...), custom_call_target="tpu_custom_call" | custom-call | bytes 4194304 | tf_op jit(solution)/shard_map/pallas_call | solution.py:94
  30.5 4.3 %collective-permute-done.6 = bf16[1024,256]{1,0:T(8,128)(2,1)S(1)} collective-permute-done((bf16[1024,256]{1,0:T(8,128)(2,1)}, bf16[1024,256]{1,0:T(8,128)(2,1)S(1)}, u32[]{:S(2)}, u32[]{:S(2)}) %collective-permute-start.6) | collective-permute-done | bytes 524320 | tf_op jit(solution)/shard_map/ppermute | solution.py:258
  38.7 21.8 %collective-permute-done.12 = bf16[512,1024]{1,0:T(8,128)(2,1)S(1)} collective-permute-done((bf16[512,1024]{1,0:T(8,128)(2,1)S(1)}, bf16[512,1024]{1,0:T(8,128)(2,1)S(1)}, u32[]{:S(2)}, u32[]{:S(2)}) %collective-permute-start.12) | collective-permute-done | bytes 1048608 | tf_op jit(solution)/shard_map/ppermute | solution.py:258
  66.2 3.5 %collective-permute-start.14 = (bf16[256,1024]{1,0:T(8,128)(2,1)S(1)}, bf16[256,1024]{1,0:T(8,128)(2,1)S(1)}, u32[]{:S(2)}, u32[]{:S(2)}) collective-permute-start(bf16[256,1024]{1,0:T(8,128)(2,1)S(1)} %convolution_convert_fusion.7), channel_id=1, source_target_pairs={{0,2},{6,4},{1,3},{7,5},{8,10},{14,12},{9,11},{15,13},{16,18},{22,... | collective-permute-start | bytes 1572872 | tf_op jit(solution)/shard_map/ppermute | solution.py:278
  71.0 4.6 %collective-permute-done.17 = bf16[1024,256]{1,0:T(8,128)(2,1)S(1)} collective-permute-done((bf16[1024,256]{1,0:T(8,128)(2,1)S(1)}, bf16[1024,256]{1,0:T(8,128)(2,1)S(1)}, u32[]{:S(2)}, u32[]{:S(2)}) %collective-permute-start.17) | collective-permute-done | bytes 524320 | tf_op jit(solution)/shard_map/ppermute | solution.py:258
  76.9 4.9 %collective-permute-done.14 = bf16[256,1024]{1,0:T(8,128)(2,1)S(1)} collective-permute-done((bf16[256,1024]{1,0:T(8,128)(2,1)S(1)}, bf16[256,1024]{1,0:T(8,128)(2,1)S(1)}, u32[]{:S(2)}, u32[]{:S(2)}) %collective-permute-start.14) | collective-permute-done | bytes 524320 | tf_op jit(solution)/shard_map/ppermute | solution.py:278
  82.0 5.2 %collective-permute-start.23 = (bf16[256,1024]{1,0:T(8,128)(2,1)S(1)}, bf16[256,1024]{1,0:T(8,128)(2,1)}, u32[]{:S(2)}, u32[]{:S(2)}) collective-permute-start(bf16[256,1024]{1,0:T(8,128)(2,1)S(1)} %convolution_convert_fusion.5), channel_id=1, source_target_pairs={{0,2},{6,4},{1,3},{7,5},{8,10},{14,12},{9,11},{15,13},{16,18},{22,... | collective-permute-start | bytes 1572872 | tf_op jit(solution)/shard_map/ppermute | solution.py:278
  93.0 5.1 %collective-permute-done.23 = bf16[256,1024]{1,0:T(8,128)(2,1)} collective-permute-done((bf16[256,1024]{1,0:T(8,128)(2,1)S(1)}, bf16[256,1024]{1,0:T(8,128)(2,1)}, u32[]{:S(2)}, u32[]{:S(2)}) %collective-permute-start.23) | collective-permute-done | bytes 524320 | tf_op jit(solution)/shard_map/ppermute | solution.py:278
  103.2 5.4 %collective-permute-start.19 = (bf16[128,1024]{1,0:T(8,128)(2,1)S(1)}, bf16[128,1024]{1,0:T(8,128)(2,1)S(1)}, u32[]{:S(2)}, u32[]{:S(2)}) collective-permute-start(bf16[128,1024]{1,0:T(8,128)(2,1)S(1)} %add_convert_fusion.8), channel_id=1, source_target_pairs={{0,2},{2,0},{4,6},{6,4},{1,3},{3,1},{5,7},{7,5},{8,10},{10,8},{12,... | collective-permute-start | bytes 786440 | tf_op jit(solution)/shard_map/ppermute | solution.py:258
  108.5 2.5 convolution_convert_fusion.4.refs_0_
  111.1 2.6 collective-permute-done.19.refs_2_
  114.4 3.6 %shard_map.96 = (bf16[128,1024]{1,0:T(8,128)(2,1)}, bf16[128,1024]{1,0:T(8,128)(2,1)}) custom-call(s32[1]{0:T(128)} %bitcast.2.place, f32[8,128]{1,0:T(8,128)} %add.78.count, bf16[256,1024]{1,0:T(8,128)(2,1)} %copy-done.9, bf16[256,1024]{1,0:T(8,128)(2,1)} %copy-done.13, bf16[128,1024]{1,0:T(8,128)(2,1)} %copy-done.29, f32[16384,128]{1,0:T(8,128)} %bitcast.64, ...), custom_call_target="tpu_custom_call" | custom-call | flops 2621440 | bytes 2621440 | tf_op jit(solution)/shard_map/pallas_call | solution.py:156
  124.1 3.6 %collective-permute-start.31 = (bf16[256,1024]{1,0:T(8,128)(2,1)S(1)}, bf16[256,1024]{1,0:T(8,128)(2,1)S(1)}, u32[]{:S(2)}, u32[]{:S(2)}) collective-permute-start(bf16[256,1024]{1,0:T(8,128)(2,1)S(1)} %convolution_convert_fusion.3), channel_id=1, source_target_pairs={{0,2},{6,4},{1,3},{7,5},{8,10},{14,12},{9,11},{15,13},{16,18},{22,... | collective-permute-start | bytes 1572872 | tf_op jit(solution)/shard_map/ppermute | solution.py:278
  133.0 10.6 %collective-permute-done.31 = bf16[256,1024]{1,0:T(8,128)(2,1)S(1)} collective-permute-done((bf16[256,1024]{1,0:T(8,128)(2,1)S(1)}, bf16[256,1024]{1,0:T(8,128)(2,1)S(1)}, u32[]{:S(2)}, u32[]{:S(2)}) %collective-permute-start.31) | collective-permute-done | bytes 524320 | tf_op jit(solution)/shard_map/ppermute | solution.py:278
  147.9 3.8 %collective-permute-done.30.refs_1_ = bf16[256,1024]{1,0:T(8,128)(2,1)S(1)} collective-permute-done((bf16[256,1024]{1,0:T(8,128)(2,1)S(1)}, bf16[256,1024]{1,0:T(8,128)(2,1)S(1)}, u32[]{:S(2)}, u32[]{:S(2)}) %collective-permute-start.30) | collective-permute-done | bytes 524320 | tf_op jit(solution)/shard_map/ppermute | solution.py:258
  154.9 4.8 %collective-permute-done.22 = bf16[256,1024]{1,0:T(8,128)(2,1)S(1)} collective-permute-done((bf16[256,1024]{1,0:T(8,128)(2,1)S(1)}, bf16[256,1024]{1,0:T(8,128)(2,1)S(1)}, u32[]{:S(2)}, u32[]{:S(2)}) %collective-permute-start.22) | collective-permute-done | bytes 524320 | tf_op jit(solution)/shard_map/ppermute | solution.py:289
  160.8 3.5 %shard_map.97 = (bf16[128,1024]{1,0:T(8,128)(2,1)}, bf16[128,1024]{1,0:T(8,128)(2,1)}) custom-call(s32[1]{0:T(128)} %bitcast.23.place, f32[8,128]{1,0:T(8,128)} %add.78.count, bf16[256,1024]{1,0:T(8,128)(2,1)} %copy-done.8, bf16[256,1024]{1,0:T(8,128)(2,1)} %copy-done.6, bf16[128,1024]{1,0:T(8,128)(2,1)} %copy-done.27, f32[16384,128]{1,0:T(8,128)} %bitcast.65, ...), custom_call_target="tpu_custom_call" | custom-call | flops 2621440 | bytes 2621440 | tf_op jit(solution)/shard_map/pallas_call | solution.py:156
  167.6 4.3 %collective-permute-done.35 = bf16[128,1024]{1,0:T(8,128)(2,1)S(1)} collective-permute-done((bf16[128,1024]{1,0:T(8,128)(2,1)}, bf16[128,1024]{1,0:T(8,128)(2,1)S(1)}, u32[]{:S(2)}, u32[]{:S(2)}) %collective-permute-start.35) | collective-permute-done | bytes 262176 | tf_op jit(solution)/shard_map/ppermute | solution.py:258
  174.6 3.5 %shard_map.99 = (bf16[128,1024]{1,0:T(8,128)(2,1)}, bf16[128,1024]{1,0:T(8,128)(2,1)}) custom-call(s32[1]{0:T(128)} %bitcast.31.place, f32[8,128]{1,0:T(8,128)} %add.78.count, bf16[256,1024]{1,0:T(8,128)(2,1)} %copy-done.12, bf16[256,1024]{1,0:T(8,128)(2,1)} %copy-done.11, bf16[128,1024]{1,0:T(8,128)(2,1)} %collective-permute-done.34.refs_2_, ...), custom_call_target="tpu_custom_call" | custom-call | flops 2621440 | bytes 2621440 | tf_op jit(solution)/shard_map/pallas_call | solution.py:156
  181.1 3.6 %shard_map.98 = (bf16[128,1024]{1,0:T(8,128)(2,1)}, bf16[128,1024]{1,0:T(8,128)(2,1)}) custom-call(s32[1]{0:T(128)} %bitcast.30.place, f32[8,128]{1,0:T(8,128)} %add.78.count, bf16[256,1024]{1,0:T(8,128)(2,1)} %copy-done.7, bf16[256,1024]{1,0:T(8,128)(2,1)} %copy-done.10, bf16[128,1024]{1,0:T(8,128)(2,1)} %copy-done.28, f32[16384,128]{1,0:T(8,128)} %bitcast.67, ...), custom_call_target="tpu_custom_call" | custom-call | flops 2621440 | bytes 2621440 | tf_op jit(solution)/shard_map/pallas_call | solution.py:156
  188.9 6.5 %collective-permute-done.38 = bf16[128,1024]{1,0:T(8,128)(2,1)S(1)} collective-permute-done((bf16[128,1024]{1,0:T(8,128)(2,1)}, bf16[128,1024]{1,0:T(8,128)(2,1)S(1)}, u32[]{:S(2)}, u32[]{:S(2)}) %collective-permute-start.38) | collective-permute-done | bytes 262176 | tf_op jit(solution)/shard_map/ppermute | solution.py:258
  198.6 2.8 %collective-permute-start.43 = (bf16[256,1024]{1,0:T(8,128)(2,1)S(1)}, bf16[256,1024]{1,0:T(8,128)(2,1)S(1)}, u32[]{:S(2)}, u32[]{:S(2)}) collective-permute-start(bf16[256,1024]{1,0:T(8,128)(2,1)S(1)} %pad_maximum_fusion.3), channel_id=1, source_target_pairs={{0,2},{2,0},{4,6},{6,4},{1,3},{3,1},{5,7},{7,5},{8,10},{10,8},{12,... | collective-permute-start | bytes 1572872 | tf_op jit(solution)/shard_map/ppermute | solution.py:258
  201.3 6.7 %fusion.8 = f32[2048,1024]{1,0:T(8,128)} fusion(bf16[1024,2048]{1,0:T(8,128)(2,1)S(1)} %constant_dynamic-update-slice_fusion.12, bf16[128,1024]{1,0:T(8,128)(2,1)S(1)} %copy-done.35, bf16[128,1024]{1,0:T(8,128)(2,1)S(1)} %collective-permute-done.39, bf16[128,1024]{1,0:T(8,128)(2,1)} %get-tuple-element.105, bf16[128,1024]{1,0:T(8,128)(2,1)S(1)} %collective-permute-done.38), kind=kOutput, calls=%fused_computation.13 | convolution fusion | flops 2151677952 | bytes 11534336 | tf_op jit(solution)/shard_map/dot_general | solution.py:391
  209.6 4.3 %collective-permute-done.37 = bf16[256,1024]{1,0:T(8,128)(2,1)S(1)} collective-permute-done((bf16[256,1024]{1,0:T(8,128)(2,1)S(1)}, bf16[256,1024]{1,0:T(8,128)(2,1)S(1)}, u32[]{:S(2)}, u32[]{:S(2)}) %collective-permute-start.37) | collective-permute-done | bytes 524320 | tf_op jit(solution)/shard_map/ppermute | solution.py:289
  214.2 7.3 %convolution_add_fusion = f32[2048,1024]{1,0:T(8,128)S(1)} fusion(f32[2048,1024]{1,0:T(8,128)} %fusion.8, bf16[1024,2048]{1,0:T(8,128)(2,1)S(1)} %copy-done.38, bf16[1024,1024]{1,0:T(8,128)(2,1)S(1)} %constant_dynamic-update-slice_fusion.24), kind=kOutput, calls=%fused_computation | convolution fusion | flops 4297064448 | bytes 23068672 | tf_op jit(solution)/shard_map/dot_general | solution.py:391
  222.7 5.1 %collective-permute-done.42 = bf16[256,1024]{1,0:T(8,128)(2,1)S(1)} collective-permute-done((bf16[256,1024]{1,0:T(8,128)(2,1)S(1)}, bf16[256,1024]{1,0:T(8,128)(2,1)S(1)}, u32[]{:S(2)}, u32[]{:S(2)}) %collective-permute-start.42) | collective-permute-done | bytes 524320 | tf_op jit(solution)/shard_map/ppermute | solution.py:289
  237.6 23.2 %shard_map.100 = (f32[16384,128]{1,0:T(8,128)}, f32[16384,128]{1,0:T(8,128)}, f32[16384,128]{1,0:T(8,128)}) custom-call(s32[1]{0:T(128)} %bitcast.place, f32[8,128]{1,0:T(8,128)} %add.78.count, bf16[512,1024]{1,0:T(8,128)(2,1)} %copy-done.4, bf16[512,1024]{1,0:T(8,128)(2,1)} %copy-done.15, bf16[512,1024]{1,0:T(8,128)(2,1)} %copy-done.14, ...), custom_call_target="tpu_custom_call" | custom-call | flops 41943040 | bytes 54525952 | tf_op jit(solution)/shard_map/pallas_call | solution.py:201
  262.4 3.8 %shard_map.101 = bf16[4096,128]{1,0:T(8,128)(2,1)} custom-call(s32[1]{0:T(128)} %bitcast.7.pair, bf16[1024,512]{1,0:T(8,128)(2,1)} %copy-done, bf16[1024,512]{1,0:T(8,128)(2,1)} %copy-done.2, bf16[512,512]{1,0:T(8,128)(2,1)} %copy-done.20, bf16[1024,512]{1,0:T(8,128)(2,1)} %copy-done.1, bf16[1024,512]{1,0:T(8,128)(2,1)} %copy-done.3, bf16[512,512]{1,0:T(8,128)(2,1)} %copy-done.21), custom_call_target="tpu_custom_call" | custom-call | bytes 4194304 | tf_op jit(solution)/shard_map/pallas_call | solution.py:238
  (224 shorter events, 86.8 us)
Async XLA Ops:
  8.9 21.6 %collective-permute-start.8 = (bf16[1024,256]{1,0:T(8,128)(2,1)}, bf16[1024,256]{1,0:T(8,128)(2,1)S(1)}, u32[]{:S(2)}, u32[]{:S(2)}) collective-permute-start(bf16[1024,256]{1,0:T(8,128)(2,1)} %get-tuple-element.65), channel_id=1, source_target_pairs={{0,1},{1,0},{2,3},{3,2},{4,5},{5,4},{6,7},{7,6},{8,9},{9,8},{10,11... | collective-permute-start | bytes 1572872 | tf_op jit(solution)/shard_map/ppermute | solution.py:258
  10.5 20.0 %collective-permute-start.9 = (bf16[1024,256]{1,0:T(8,128)(2,1)}, bf16[1024,256]{1,0:T(8,128)(2,1)S(1)}, u32[]{:S(2)}, u32[]{:S(2)}) collective-permute-start(bf16[1024,256]{1,0:T(8,128)(2,1)} %get-tuple-element.67), channel_id=1, source_target_pairs={{0,16},{8,24},{16,0},{24,8},{1,17},{9,25},{17,1},{25,9},{2,18},{10... | collective-permute-start | bytes 1572872 | tf_op jit(solution)/shard_map/ppermute | solution.py:258
  12.5 22.3 %collective-permute-start.6 = (bf16[1024,256]{1,0:T(8,128)(2,1)}, bf16[1024,256]{1,0:T(8,128)(2,1)S(1)}, u32[]{:S(2)}, u32[]{:S(2)}) collective-permute-start(bf16[1024,256]{1,0:T(8,128)(2,1)} %get-tuple-element.62), channel_id=1, source_target_pairs={{0,24},{8,16},{16,8},{24,0},{1,25},{9,17},{17,9},{25,1},{2,26},{10... | collective-permute-start | bytes 1572872 | tf_op jit(solution)/shard_map/ppermute | solution.py:258
  12.5 22.2 %collective-permute-start.5 = (bf16[1024,256]{1,0:T(8,128)(2,1)S(1)}, bf16[1024,256]{1,0:T(8,128)(2,1)S(1)}, u32[]{:S(2)}, u32[]{:S(2)}) collective-permute-start(bf16[1024,256]{1,0:T(8,128)(2,1)S(1)} %collective-permute-done.4), channel_id=1, source_target_pairs={{0,1},{1,0},{2,3},{3,2},{4,5},{5,4},{6,7},{7,6},{8,9},{9,8},{10,11... | collective-permute-start | bytes 1572872 | tf_op jit(solution)/shard_map/ppermute | solution.py:258
  34.8 25.7 %collective-permute-start.12 = (bf16[512,1024]{1,0:T(8,128)(2,1)S(1)}, bf16[512,1024]{1,0:T(8,128)(2,1)S(1)}, u32[]{:S(2)}, u32[]{:S(2)}) collective-permute-start(bf16[512,1024]{1,0:T(8,128)(2,1)S(1)} %copy-done.16), channel_id=1, source_target_pairs={{0,16},{8,24},{16,0},{24,8},{1,17},{9,25},{17,1},{25,9},{2,18},{10... | collective-permute-start | bytes 3145736 | tf_op jit(solution)/shard_map/ppermute | solution.py:258
  35.5 25.3 %collective-permute-start.11 = (bf16[512,1024]{1,0:T(8,128)(2,1)S(1)}, bf16[512,1024]{1,0:T(8,128)(2,1)S(1)}, u32[]{:S(2)}, u32[]{:S(2)}) collective-permute-start(bf16[512,1024]{1,0:T(8,128)(2,1)S(1)} %copy-done.16), channel_id=1, source_target_pairs={{0,8},{8,0},{16,24},{24,16},{1,9},{9,1},{17,25},{25,17},{2,10},{10... | collective-permute-start | bytes 3145736 | tf_op jit(solution)/shard_map/ppermute | solution.py:258
  36.7 24.1 %collective-permute-start.10 = (bf16[1024,256]{1,0:T(8,128)(2,1)S(1)}, bf16[1024,256]{1,0:T(8,128)(2,1)S(1)}, u32[]{:S(2)}, u32[]{:S(2)}) collective-permute-start(bf16[1024,256]{1,0:T(8,128)(2,1)S(1)} %collective-permute-done.9), channel_id=1, source_target_pairs={{0,1},{1,0},{2,3},{3,2},{4,5},{5,4},{6,7},{7,6},{8,9},{9,8},{10,11... | collective-permute-start | bytes 1572872 | tf_op jit(solution)/shard_map/ppermute | solution.py:258
  38.2 24.2 %collective-permute-start.26 = (bf16[1024,256]{1,0:T(8,128)(2,1)}, bf16[1024,256]{1,0:T(8,128)(2,1)}, u32[]{:S(2)}, u32[]{:S(2)}) collective-permute-start(bf16[1024,256]{1,0:T(8,128)(2,1)} %get-tuple-element.71), channel_id=1, source_target_pairs={{0,8},{8,0},{16,24},{24,16},{1,9},{9,1},{17,25},{25,17},{2,10},{10... | collective-permute-start | bytes 1572872 | tf_op jit(solution)/shard_map/ppermute | solution.py:258
  38.2 24.2 %collective-permute-start.7 = (bf16[1024,256]{1,0:T(8,128)(2,1)S(1)}, bf16[1024,256]{1,0:T(8,128)(2,1)S(1)}, u32[]{:S(2)}, u32[]{:S(2)}) collective-permute-start(bf16[1024,256]{1,0:T(8,128)(2,1)S(1)} %collective-permute-done.6), channel_id=1, source_target_pairs={{0,1},{1,0},{2,3},{3,2},{4,5},{5,4},{6,7},{7,6},{8,9},{9,8},{10,11... | collective-permute-start | bytes 1572872 | tf_op jit(solution)/shard_map/ppermute | solution.py:258
  62.4 28.4 %collective-permute-start.27 = (bf16[1024,256]{1,0:T(8,128)(2,1)}, bf16[1024,256]{1,0:T(8,128)(2,1)}, u32[]{:S(2)}, u32[]{:S(2)}) collective-permute-start(bf16[1024,256]{1,0:T(8,128)(2,1)} %collective-permute-done.26), channel_id=1, source_target_pairs={{0,1},{1,0},{2,3},{3,2},{4,5},{5,4},{6,7},{7,6},{8,9},{9,8},{10,11... | collective-permute-start | bytes 1572872 | tf_op jit(solution)/shard_map/ppermute | solution.py:258
  63.6 24.4 %collective-permute-start.16 = (bf16[1024,256]{1,0:T(8,128)(2,1)}, bf16[1024,256]{1,0:T(8,128)(2,1)S(1)}, u32[]{:S(2)}, u32[]{:S(2)}) collective-permute-start(bf16[1024,256]{1,0:T(8,128)(2,1)} %get-tuple-element.76), channel_id=1, source_target_pairs={{0,16},{8,24},{16,0},{24,8},{1,17},{9,25},{17,1},{25,9},{2,18},{10... | collective-permute-start | bytes 1572872 | tf_op jit(solution)/shard_map/ppermute | solution.py:258
  64.5 27.4 %collective-permute-start.24 = (bf16[1024,256]{1,0:T(8,128)(2,1)}, bf16[1024,256]{1,0:T(8,128)(2,1)}, u32[]{:S(2)}, u32[]{:S(2)}) collective-permute-start(bf16[1024,256]{1,0:T(8,128)(2,1)} %get-tuple-element.87), channel_id=1, source_target_pairs={{0,24},{8,16},{16,8},{24,0},{1,25},{9,17},{17,9},{25,1},{2,26},{10... | collective-permute-start | bytes 1572872 | tf_op jit(solution)/shard_map/ppermute | solution.py:258
  66.2 15.6 %collective-permute-start.14 = (bf16[256,1024]{1,0:T(8,128)(2,1)S(1)}, bf16[256,1024]{1,0:T(8,128)(2,1)S(1)}, u32[]{:S(2)}, u32[]{:S(2)}) collective-permute-start(bf16[256,1024]{1,0:T(8,128)(2,1)S(1)} %convolution_convert_fusion.7), channel_id=1, source_target_pairs={{0,2},{6,4},{1,3},{7,5},{8,10},{14,12},{9,11},{15,13},{16,18},{22,... | collective-permute-start | bytes 1572872 | tf_op jit(solution)/shard_map/ppermute | solution.py:278
  82.0 16.2 %collective-permute-start.23 = (bf16[256,1024]{1,0:T(8,128)(2,1)S(1)}, bf16[256,1024]{1,0:T(8,128)(2,1)}, u32[]{:S(2)}, u32[]{:S(2)}) collective-permute-start(bf16[256,1024]{1,0:T(8,128)(2,1)S(1)} %convolution_convert_fusion.5), channel_id=1, source_target_pairs={{0,2},{6,4},{1,3},{7,5},{8,10},{14,12},{9,11},{15,13},{16,18},{22,... | collective-permute-start | bytes 1572872 | tf_op jit(solution)/shard_map/ppermute | solution.py:278
  87.2 15.1 %collective-permute-start.15 = (bf16[256,1024]{1,0:T(8,128)(2,1)S(1)}, bf16[256,1024]{1,0:T(8,128)(2,1)S(1)}, u32[]{:S(2)}, u32[]{:S(2)}) collective-permute-start(bf16[256,1024]{1,0:T(8,128)(2,1)S(1)} %add_convert_fusion.4), channel_id=1, source_target_pairs={{2,4},{4,2},{3,5},{5,3},{10,12},{12,10},{11,13},{13,11},{18,20},{2... | collective-permute-start | bytes 1572872 | tf_op jit(solution)/shard_map/ppermute | solution.py:282
  100.2 20.6 %collective-permute-start.25 = (bf16[256,1024]{1,0:T(8,128)(2,1)}, bf16[256,1024]{1,0:T(8,128)(2,1)S(1)}, u32[]{:S(2)}, u32[]{:S(2)}) collective-permute-start(bf16[256,1024]{1,0:T(8,128)(2,1)} %add_convert_fusion.3), channel_id=1, source_target_pairs={{2,4},{4,2},{3,5},{5,3},{10,12},{12,10},{11,13},{13,11},{18,20},{2... | collective-permute-start | bytes 1572872 | tf_op jit(solution)/shard_map/ppermute | solution.py:282
  101.1 19.7 %collective-permute-start.28 = (bf16[1024,256]{1,0:T(8,128)(2,1)}, bf16[1024,256]{1,0:T(8,128)(2,1)}, u32[]{:S(2)}, u32[]{:S(2)}) collective-permute-start(bf16[1024,256]{1,0:T(8,128)(2,1)} %collective-permute-done.24), channel_id=1, source_target_pairs={{0,1},{1,0},{2,3},{3,2},{4,5},{5,4},{6,7},{7,6},{8,9},{9,8},{10,11... | collective-permute-start | bytes 1572872 | tf_op jit(solution)/shard_map/ppermute | solution.py:258
  120.8 27.0 %collective-permute-start.29 = (bf16[128,1024]{1,0:T(8,128)(2,1)S(1)}, bf16[128,1024]{1,0:T(8,128)(2,1)S(1)}, u32[]{:S(2)}, u32[]{:S(2)}) collective-permute-start(bf16[128,1024]{1,0:T(8,128)(2,1)S(1)} %add_convert_fusion.7), channel_id=1, source_target_pairs={{0,2},{2,0},{4,6},{6,4},{1,3},{3,1},{5,7},{7,5},{8,10},{10,8},{12,... | collective-permute-start | bytes 786440 | tf_op jit(solution)/shard_map/ppermute | solution.py:258
  124.1 19.5 %collective-permute-start.31 = (bf16[256,1024]{1,0:T(8,128)(2,1)S(1)}, bf16[256,1024]{1,0:T(8,128)(2,1)S(1)}, u32[]{:S(2)}, u32[]{:S(2)}) collective-permute-start(bf16[256,1024]{1,0:T(8,128)(2,1)S(1)} %convolution_convert_fusion.3), channel_id=1, source_target_pairs={{0,2},{6,4},{1,3},{7,5},{8,10},{14,12},{9,11},{15,13},{16,18},{22,... | collective-permute-start | bytes 1572872 | tf_op jit(solution)/shard_map/ppermute | solution.py:278
  129.1 16.1 %collective-permute-start.21 = (bf16[256,1024]{1,0:T(8,128)(2,1)S(1)}, bf16[256,1024]{1,0:T(8,128)(2,1)S(1)}, u32[]{:S(2)}, u32[]{:S(2)}) collective-permute-start(bf16[256,1024]{1,0:T(8,128)(2,1)S(1)} %pad_maximum_fusion), channel_id=1, source_target_pairs={{2,4},{4,2},{3,5},{5,3},{10,12},{12,10},{11,13},{13,11},{18,20},{2... | collective-permute-start | bytes 1572872 | tf_op jit(solution)/shard_map/ppermute | solution.py:288
  131.2 20.5 %collective-permute-start.30 = (bf16[256,1024]{1,0:T(8,128)(2,1)S(1)}, bf16[256,1024]{1,0:T(8,128)(2,1)S(1)}, u32[]{:S(2)}, u32[]{:S(2)}) collective-permute-start(bf16[256,1024]{1,0:T(8,128)(2,1)S(1)} %convolution_convert_fusion.1), channel_id=1, source_target_pairs={{0,2},{2,0},{4,6},{6,4},{1,3},{3,1},{5,7},{7,5},{8,10},{10,8},{12,... | collective-permute-start | bytes 1572872 | tf_op jit(solution)/shard_map/ppermute | solution.py:258
  144.6 19.8 %collective-permute-start.32 = (bf16[256,1024]{1,0:T(8,128)(2,1)}, bf16[256,1024]{1,0:T(8,128)(2,1)S(1)}, u32[]{:S(2)}, u32[]{:S(2)}) collective-permute-start(bf16[256,1024]{1,0:T(8,128)(2,1)} %add_convert_fusion.2), channel_id=1, source_target_pairs={{2,4},{4,2},{3,5},{5,3},{10,12},{12,10},{11,13},{13,11},{18,20},{2... | collective-permute-start | bytes 1572872 | tf_op jit(solution)/shard_map/ppermute | solution.py:282
  152.5 22.0 %collective-permute-start.34 = (bf16[128,1024]{1,0:T(8,128)(2,1)}, bf16[128,1024]{1,0:T(8,128)(2,1)}, u32[]{:S(2)}, u32[]{:S(2)}) collective-permute-start(bf16[128,1024]{1,0:T(8,128)(2,1)} %add_convert_fusion.6), channel_id=1, source_target_pairs={{0,4},{2,6},{4,0},{6,2},{1,5},{3,7},{5,1},{7,3},{8,12},{10,14},{12... | collective-permute-start | bytes 786440 | tf_op jit(solution)/shard_map/ppermute | solution.py:258
  164.5 15.9 %collective-permute-start.33 = (bf16[128,1024]{1,0:T(8,128)(2,1)S(1)}, bf16[128,1024]{1,0:T(8,128)(2,1)S(1)}, u32[]{:S(2)}, u32[]{:S(2)}) collective-permute-start(bf16[128,1024]{1,0:T(8,128)(2,1)S(1)} %add_convert_fusion.5), channel_id=1, source_target_pairs={{0,2},{2,0},{4,6},{6,4},{1,3},{3,1},{5,7},{7,5},{8,10},{10,8},{12,... | collective-permute-start | bytes 786440 | tf_op jit(solution)/shard_map/ppermute | solution.py:258
  172.9 24.2 %collective-permute-start.36 = (bf16[256,1024]{1,0:T(8,128)(2,1)S(1)}, bf16[256,1024]{1,0:T(8,128)(2,1)S(1)}, u32[]{:S(2)}, u32[]{:S(2)}) collective-permute-start(bf16[256,1024]{1,0:T(8,128)(2,1)S(1)} %pad_maximum_fusion.1), channel_id=1, source_target_pairs={{2,4},{4,2},{3,5},{5,3},{10,12},{12,10},{11,13},{13,11},{18,20},{2... | collective-permute-start | bytes 1572872 | tf_op jit(solution)/shard_map/ppermute | solution.py:288
  178.1 20.4 %collective-permute-start.39 = (bf16[128,1024]{1,0:T(8,128)(2,1)}, bf16[128,1024]{1,0:T(8,128)(2,1)S(1)}, u32[]{:S(2)}, u32[]{:S(2)}) collective-permute-start(bf16[128,1024]{1,0:T(8,128)(2,1)} %get-tuple-element.106), channel_id=1, source_target_pairs={{0,4},{2,6},{4,0},{6,2},{1,5},{3,7},{5,1},{7,3},{8,12},{10,14},{12... | collective-permute-start | bytes 786440 | tf_op jit(solution)/shard_map/ppermute | solution.py:258
  186.5 35.0 %collective-permute-start.40 = (bf16[512,1024]{1,0:T(8,128)(2,1)S(1)}, bf16[512,1024]{1,0:T(8,128)(2,1)S(1)}, u32[]{:S(2)}, u32[]{:S(2)}) collective-permute-start(bf16[512,1024]{1,0:T(8,128)(2,1)S(1)} %constant_dynamic-update-slice_fusion.20.refs_0_), channel_id=1, source_target_pairs={{0,16},{8,24},{16,0},{24,8},{1,17},{9,25},{17,1},{25,9},{2,18},{10... | collective-permute-start | bytes 3145736 | tf_op jit(solution)/shard_map/ppermute | solution.py:258
  197.2 16.8 %collective-permute-start.37 = (bf16[256,1024]{1,0:T(8,128)(2,1)S(1)}, bf16[256,1024]{1,0:T(8,128)(2,1)S(1)}, u32[]{:S(2)}, u32[]{:S(2)}) collective-permute-start(bf16[256,1024]{1,0:T(8,128)(2,1)S(1)} %collective-permute-done.36), channel_id=1, source_target_pairs={{2,0},{4,6},{3,1},{5,7},{10,8},{12,14},{11,9},{13,15},{18,16},{20,... | collective-permute-start | bytes 1572872 | tf_op jit(solution)/shard_map/ppermute | solution.py:289
  198.6 23.6 %collective-permute-start.43 = (bf16[256,1024]{1,0:T(8,128)(2,1)S(1)}, bf16[256,1024]{1,0:T(8,128)(2,1)S(1)}, u32[]{:S(2)}, u32[]{:S(2)}) collective-permute-start(bf16[256,1024]{1,0:T(8,128)(2,1)S(1)} %pad_maximum_fusion.3), channel_id=1, source_target_pairs={{0,2},{2,0},{4,6},{6,4},{1,3},{3,1},{5,7},{7,5},{8,10},{10,8},{12,... | collective-permute-start | bytes 1572872 | tf_op jit(solution)/shard_map/ppermute | solution.py:258
  208.1 19.8 %collective-permute-start.42 = (bf16[256,1024]{1,0:T(8,128)(2,1)S(1)}, bf16[256,1024]{1,0:T(8,128)(2,1)S(1)}, u32[]{:S(2)}, u32[]{:S(2)}) collective-permute-start(bf16[256,1024]{1,0:T(8,128)(2,1)S(1)} %collective-permute-done.41), channel_id=1, source_target_pairs={{2,0},{4,6},{3,1},{5,7},{10,8},{12,14},{11,9},{13,15},{18,16},{20,... | collective-permute-start | bytes 1572872 | tf_op jit(solution)/shard_map/ppermute | solution.py:289
  232.7 28.1 %collective-permute-start.48 = (bf16[512,512]{1,0:T(8,128)(2,1)S(1)}, bf16[512,512]{1,0:T(8,128)(2,1)S(1)}, u32[]{:S(2)}, u32[]{:S(2)}) collective-permute-start(bf16[512,512]{1,0:T(8,128)(2,1)S(1)} %add_convert_fusion), channel_id=1, source_target_pairs={{0,16},{8,24},{16,0},{24,8},{1,17},{9,25},{17,1},{25,9},{2,18},{10... | collective-permute-start | bytes 1572872 | tf_op jit(solution)/shard_map/ppermute | solution.py:258
  235.9 24.9 %collective-permute-start.49 = (bf16[512,512]{1,0:T(8,128)(2,1)S(1)}, bf16[512,512]{1,0:T(8,128)(2,1)S(1)}, u32[]{:S(2)}, u32[]{:S(2)}) collective-permute-start(bf16[512,512]{1,0:T(8,128)(2,1)S(1)} %add_convert_fusion.1), channel_id=1, source_target_pairs={{0,16},{8,24},{16,0},{24,8},{1,17},{9,25},{17,1},{25,9},{2,18},{10... | collective-permute-start | bytes 1572872 | tf_op jit(solution)/shard_map/ppermute | solution.py:258
  (57 other events, 590.8 us)
where the time goes:
time: 267 us; the launch traced here: 266 us
  waiting for transfers between devices  86.5 us (32%)
  starting transfers between devices  70.5 us (26%)
  Pallas kernels  52.1 us (20%)
  matrix products  29.4 us (11%)
  local copies, waits for them, and re-layouts  16.3 us (6%)
  other arithmetic  9.08 us (3%)
    ppermute x38, waiting for transfers between devices, swap(): lax.ppermute(value, axis, [(i, i ^ k) for i in range(lax.axis_size(axis))])  51.6 us
    ppermute x38, starting transfers between devices, swap(): lax.ppermute(value, axis, [(i, i ^ k) for i in range(lax.axis_size(axis))])  49.4 us
    pallas_call x1, Pallas kernels, update(): call(kernel, [jax.ShapeDtypeStruct(params[0].shape, jnp.float32)] * 3, 20...  23.2 us
    ppermute x3, waiting for transfers between devices, send(): lax.ppermute(away, 'shard', self.ends_to_inner)  20.6 us
    dot_general x10, matrix products, project(): lax.dot_general(rows, weights, by_rows, preferred_element_type=jnp.float32)  17.9 us
    unnamed x100, local copies, waits for them, and re-layouts  14.6 us
    ppermute x3, waiting for transfers between devices, gather(): far = lax.ppermute(got, 'shard', self.inner_to_ends)  14.3 us
    pallas_call x4, Pallas kernels, fresh_weights(): call(kernel, [jax.ShapeDtypeStruct((part, width), jnp.bfloat16)] * 2, 20...  14.2 us
  transfers between devices with their start and end apart: 50, of which 17 were waited for; matrix products, arithmetic and copies ran while one was open for 18% of the time, Pallas kernels for 17%

commit v1 on v0

--- a/solution.py
+++ b/solution.py
@@ -315,6 +315,7 @@
         blocks, k = own, self.shards // 2
         while k > 1:
             blocks, k = jnp.concatenate([swap(blocks, "shard", k), blocks], axis=0), k // 2
+        blocks = after(blocks, *waits)
         return [swap(blocks, "shard", 1), blocks]
 
 
@@ -440,7 +441,7 @@
             fresh.append(weights)
             grads.append(grad)
             if n + 1 == len(loads) or inside == 0:
-                gathered.append(ways[g].gather(weights))
+                gathered.append(ways[g].gather(weights, *(gathered[1][:1] if n and inside else [])))
             if n and inside == 0:
                 gathered.insert(1, ways[1].gather(fresh[1], steps[2]))
         inputs.append(laid)

time: 267 us -> 270 us (1.011)
    ppermute x38, waiting for transfers between devices: 51.6 us -> 68.4 us  [swap(): lax.ppermute(value, axis, [(i, i ^ k) for i in range(lax.axis_size(axis))])]
    ppermute x3, waiting for transfers between devices: 20.6 us -> 12.9 us  [send(): lax.ppermute(away, 'shard', self.ends_to_inner)]
    ppermute x3, waiting for transfers between devices: 14.3 us -> 7.68 us  [gather(): far = lax.ppermute(got, 'shard', self.inner_to_ends)]
    ppermute x38, starting transfers between devices: 49.4 us -> 46.4 us  [swap(): lax.ppermute(value, axis, [(i, i ^ k) for i in range(lax.axis_size(axis))])]
    unnamed x100 -> x110, local copies, waits for them, and re-layouts: 14.6 us -> 13.9 us
  transfers between devices with their start and end apart: 50 -> 50, of which waited for: 17 -> 21; matrix products, arithmetic and copies ran while one was open for 18% -> 18% of each run, Pallas kernels for 17% -> 17%
where the time goes in v1:
time: 270 us; the launch traced here: 269 us
  waiting for transfers between devices  89 us (33%)
  starting transfers between devices  68.5 us (25%)
  Pallas kernels  52.1 us (19%)
  matrix products  31.6 us (12%)
  local copies, waits for them, and re-layouts  17.3 us (6%)
  other arithmetic  8.35 us (3%)
    ppermute x38, waiting for transfers between devices, swap(): lax.ppermute(value, axis, [(i, i ^ k) for i in range(lax.axis_size(axis))])  68.4 us
    ppermute x38, starting transfers between devices, swap(): lax.ppermute(value, axis, [(i, i ^ k) for i in range(lax.axis_size(axis))])  46.4 us
    pallas_call x1, Pallas kernels, update(): call(kernel, [jax.ShapeDtypeStruct(params[0].shape, jnp.float32)] * 3, 20...  23.2 us
    dot_general x10, matrix products, project(): lax.dot_general(rows, weights, by_rows, preferred_element_type=jnp.float32)  17.1 us
    pallas_call x4, Pallas kernels, fresh_weights(): call(kernel, [jax.ShapeDtypeStruct((part, width), jnp.bfloat16)] * 2, 20...  14.1 us
    unnamed x110, local copies, waits for them, and re-layouts  13.9 us
    ppermute x3, waiting for transfers between devices, send(): lax.ppermute(away, 'shard', self.ends_to_inner)  12.9 us
    ppermute x3, starting transfers between devices, send(): lax.ppermute(away, 'shard', self.ends_to_inner)  12.8 us
  transfers between devices with their start and end apart: 50, of which 21 were waited for; matrix products, arithmetic and copies ran while one was open for 18% of the time, Pallas kernels for 17%

profile of v1, /device:TPU:0, one launch (start us, length us, event | category | flops | bytes accessed | tf_op | source)
XLA Modules:
  0.0 269.1 jit_solution(2554918238994309945)
XLA Ops:
  1.3 3.8 %shard_map.93 = (bf16[1024,256]{1,0:T(8,128)(2,1)}, bf16[1024,256]{1,0:T(8,128)(2,1)}, bf16[1024,256]{1,0:T(8,128)(2,1)}, bf16[1024,256]{1,0:T(8,128)(2,1)}) custom-call(s32[9]{0:T(128)} %stack.48.place, bf16[256,8192]{1,0:T(8,128)(2,1)} %refs_31_.3, bf16[256,8192]{1,0:T(8,128)(2,1)} %refs_31_.3, bf16[256,8192]{1,0:T(8,128)(2,1)} %refs_31_.3, ...), custom_call_target="tpu_custom_call" | custom-call | bytes 4194304 | tf_op jit(solution)/shard_map/pallas_call | solution.py:94
  6.2 2.6 collective-permute-start
  18.7 2.6 collective-permute-start.3
  22.0 3.2 %shard_map.94 = (bf16[512,1024]{1,0:T(8,128)(2,1)}, f32[8,128]{1,0:T(8,128)}) custom-call(s32[2]{0:T(128)} %pad_add_fusion.place, bf16[4096,128]{1,0:T(8,128)(2,1)} %bitcast.80), custom_call_target="tpu_custom_call" | custom-call | bytes 2097152 | tf_op jit(solution)/shard_map/pallas_call | solution.py:126
  26.4 4.0 %shard_map.95 = (bf16[1024,256]{1,0:T(8,128)(2,1)}, bf16[1024,256]{1,0:T(8,128)(2,1)}, bf16[1024,256]{1,0:T(8,128)(2,1)}, bf16[1024,256]{1,0:T(8,128)(2,1)}) custom-call(s32[9]{0:T(128)} %stack.54.place, bf16[256,8192]{1,0:T(8,128)(2,1)} %refs_31_.3, bf16[256,8192]{1,0:T(8,128)(2,1)} %refs_31_.3, bf16[256,8192]{1,0:T(8,128)(2,1)} %refs_31_.3, ...), custom_call_target="tpu_custom_call" | custom-call | bytes 4194304 | tf_op jit(solution)/shard_map/pallas_call | solution.py:94
  30.4 4.2 %collective-permute-done.6 = bf16[1024,256]{1,0:T(8,128)(2,1)S(1)} collective-permute-done((bf16[1024,256]{1,0:T(8,128)(2,1)}, bf16[1024,256]{1,0:T(8,128)(2,1)S(1)}, u32[]{:S(2)}, u32[]{:S(2)}) %collective-permute-start.6) | collective-permute-done | bytes 524320 | tf_op jit(solution)/shard_map/ppermute | solution.py:258
  38.6 21.8 %collective-permute-done.12 = bf16[512,1024]{1,0:T(8,128)(2,1)S(1)} collective-permute-done((bf16[512,1024]{1,0:T(8,128)(2,1)S(1)}, bf16[512,1024]{1,0:T(8,128)(2,1)S(1)}, u32[]{:S(2)}, u32[]{:S(2)}) %collective-permute-start.12) | collective-permute-done | bytes 1048608 | tf_op jit(solution)/shard_map/ppermute | solution.py:258
  66.1 3.5 %collective-permute-start.14 = (bf16[256,1024]{1,0:T(8,128)(2,1)S(1)}, bf16[256,1024]{1,0:T(8,128)(2,1)S(1)}, u32[]{:S(2)}, u32[]{:S(2)}) collective-permute-start(bf16[256,1024]{1,0:T(8,128)(2,1)S(1)} %convolution_convert_fusion.7), channel_id=1, source_target_pairs={{0,2},{6,4},{1,3},{7,5},{8,10},{14,12},{9,11},{15,13},{16,18},{22,... | collective-permute-start | bytes 1572872 | tf_op jit(solution)/shard_map/ppermute | solution.py:278
  71.0 4.6 %collective-permute-done.17 = bf16[1024,256]{1,0:T(8,128)(2,1)S(1)} collective-permute-done((bf16[1024,256]{1,0:T(8,128)(2,1)S(1)}, bf16[1024,256]{1,0:T(8,128)(2,1)S(1)}, u32[]{:S(2)}, u32[]{:S(2)}) %collective-permute-start.17) | collective-permute-done | bytes 524320 | tf_op jit(solution)/shard_map/ppermute | solution.py:258
  76.8 4.9 %collective-permute-done.14 = bf16[256,1024]{1,0:T(8,128)(2,1)S(1)} collective-permute-done((bf16[256,1024]{1,0:T(8,128)(2,1)S(1)}, bf16[256,1024]{1,0:T(8,128)(2,1)S(1)}, u32[]{:S(2)}, u32[]{:S(2)}) %collective-permute-start.14) | collective-permute-done | bytes 524320 | tf_op jit(solution)/shard_map/ppermute | solution.py:278
  82.0 4.4 %collective-permute-start.23 = (bf16[256,1024]{1,0:T(8,128)(2,1)S(1)}, bf16[256,1024]{1,0:T(8,128)(2,1)S(1)}, u32[]{:S(2)}, u32[]{:S(2)}) collective-permute-start(bf16[256,1024]{1,0:T(8,128)(2,1)S(1)} %convolution_convert_fusion.5), channel_id=1, source_target_pairs={{0,2},{6,4},{1,3},{7,5},{8,10},{14,12},{9,11},{15,13},{16,18},{22,... | collective-permute-start | bytes 1572872 | tf_op jit(solution)/shard_map/ppermute | solution.py:278
  92.2 5.9 %collective-permute-done.23 = bf16[256,1024]{1,0:T(8,128)(2,1)S(1)} collective-permute-done((bf16[256,1024]{1,0:T(8,128)(2,1)S(1)}, bf16[256,1024]{1,0:T(8,128)(2,1)S(1)}, u32[]{:S(2)}, u32[]{:S(2)}) %collective-permute-start.23) | collective-permute-done | bytes 524320 | tf_op jit(solution)/shard_map/ppermute | solution.py:278
  102.3 4.8 %collective-permute-start.19 = (bf16[128,1024]{1,0:T(8,128)(2,1)S(1)}, bf16[128,1024]{1,0:T(8,128)(2,1)S(1)}, u32[]{:S(2)}, u32[]{:S(2)}) collective-permute-start(bf16[128,1024]{1,0:T(8,128)(2,1)S(1)} %add_convert_fusion.8), channel_id=1, source_target_pairs={{0,2},{2,0},{4,6},{6,4},{1,3},{3,1},{5,7},{7,5},{8,10},{10,8},{12,... | collective-permute-start | bytes 786440 | tf_op jit(solution)/shard_map/ppermute | solution.py:258
  109.7 2.6 collective-permute-done.19.refs_2_
  113.0 3.6 %shard_map.96 = (bf16[128,1024]{1,0:T(8,128)(2,1)}, bf16[128,1024]{1,0:T(8,128)(2,1)}) custom-call(s32[1]{0:T(128)} %bitcast.2.place, f32[8,128]{1,0:T(8,128)} %add.78.count, bf16[256,1024]{1,0:T(8,128)(2,1)} %copy-done.10, bf16[256,1024]{1,0:T(8,128)(2,1)} %copy-done.13, bf16[128,1024]{1,0:T(8,128)(2,1)} %copy-done.31, f32[16384,128]{1,0:T(8,128)} %bitcast.64, ...), custom_call_target="tpu_custom_call" | custom-call | flops 2621440 | bytes 2621440 | tf_op jit(solution)/shard_map/pallas_call | solution.py:156
  120.3 5.7 %collective-permute-done.20 = bf16[128,1024]{1,0:T(8,128)(2,1)S(1)} collective-permute-done((bf16[128,1024]{1,0:T(8,128)(2,1)}, bf16[128,1024]{1,0:T(8,128)(2,1)S(1)}, u32[]{:S(2)}, u32[]{:S(2)}) %collective-permute-start.20) | collective-permute-done | bytes 262176 | tf_op jit(solution)/shard_map/ppermute | solution.py:258
  128.2 4.9 %collective-permute-start.31 = (bf16[256,1024]{1,0:T(8,128)(2,1)S(1)}, bf16[256,1024]{1,0:T(8,128)(2,1)S(1)}, u32[]{:S(2)}, u32[]{:S(2)}) collective-permute-start(bf16[256,1024]{1,0:T(8,128)(2,1)S(1)} %convolution_convert_fusion.3), channel_id=1, source_target_pairs={{0,2},{6,4},{1,3},{7,5},{8,10},{14,12},{9,11},{15,13},{16,18},{22,... | collective-permute-start | bytes 1572872 | tf_op jit(solution)/shard_map/ppermute | solution.py:278
  137.8 4.2 %collective-permute-start.30 = (bf16[256,1024]{1,0:T(8,128)(2,1)}, bf16[256,1024]{1,0:T(8,128)(2,1)S(1)}, u32[]{:S(2)}, u32[]{:S(2)}) collective-permute-start(bf16[256,1024]{1,0:T(8,128)(2,1)} %convolution_convert_fusion.1), channel_id=1, source_target_pairs={{0,2},{2,0},{4,6},{6,4},{1,3},{3,1},{5,7},{7,5},{8,10},{10,8},{12,... | collective-permute-start | bytes 1572872 | tf_op jit(solution)/shard_map/ppermute | solution.py:258
  145.0 7.7 %collective-permute-done.22 = bf16[256,1024]{1,0:T(8,128)(2,1)S(1)} collective-permute-done((bf16[256,1024]{1,0:T(8,128)(2,1)S(1)}, bf16[256,1024]{1,0:T(8,128)(2,1)S(1)}, u32[]{:S(2)}, u32[]{:S(2)}) %collective-permute-start.22) | collective-permute-done | bytes 524320 | tf_op jit(solution)/shard_map/ppermute | solution.py:289
  154.4 3.5 %shard_map.97 = (bf16[128,1024]{1,0:T(8,128)(2,1)}, bf16[128,1024]{1,0:T(8,128)(2,1)}) custom-call(s32[1]{0:T(128)} %bitcast.23.place, f32[8,128]{1,0:T(8,128)} %add.78.count, bf16[256,1024]{1,0:T(8,128)(2,1)} %copy-done.9, bf16[256,1024]{1,0:T(8,128)(2,1)} %copy-done.7, bf16[128,1024]{1,0:T(8,128)(2,1)} %copy-done.28, f32[16384,128]{1,0:T(8,128)} %bitcast.65, ...), custom_call_target="tpu_custom_call" | custom-call | flops 2621440 | bytes 2621440 | tf_op jit(solution)/shard_map/pallas_call | solution.py:156
  157.9 3.5 %convolution_convert_fusion.refs_0_ = bf16[256,1024]{1,0:T(8,128)(2,1)S(1)} fusion(bf16[2048,1024]{1,0:T(8,128)(2,1)} %copy-done.32, bf16[1024,2048]{1,0:T(8,128)(2,1)S(1)} %constant_dynamic-update-slice_fusion.12), kind=kOutput, calls=%fused_computation.15 | convolution fusion | flops 1074003968 | bytes 5767168 | tf_op jit(solution)/shard_map/dot_general | solution.py:411
  166.2 5.4 %collective-permute-done.33.refs_2_ = bf16[128,1024]{1,0:T(8,128)(2,1)S(1)} collective-permute-done((bf16[128,1024]{1,0:T(8,128)(2,1)S(1)}, bf16[128,1024]{1,0:T(8,128)(2,1)S(1)}, u32[]{:S(2)}, u32[]{:S(2)}) %collective-permute-start.33) | collective-permute-done | bytes 262176 | tf_op jit(solution)/shard_map/ppermute | solution.py:258
  172.3 3.5 %shard_map.98 = (bf16[128,1024]{1,0:T(8,128)(2,1)}, bf16[128,1024]{1,0:T(8,128)(2,1)}) custom-call(s32[1]{0:T(128)} %bitcast.30.place, f32[8,128]{1,0:T(8,128)} %add.78.count, bf16[256,1024]{1,0:T(8,128)(2,1)} %copy-done.12, bf16[256,1024]{1,0:T(8,128)(2,1)} %copy-done.14, bf16[128,1024]{1,0:T(8,128)(2,1)} %copy-done.30, f32[16384,128]{1,0:T(8,128)} %bitcast.66, ...), custom_call_target="tpu_custom_call" | custom-call | flops 2621440 | bytes 2621440 | tf_op jit(solution)/shard_map/pallas_call | solution.py:156
  179.0 6.5 %collective-permute-done.38 = bf16[128,1024]{1,0:T(8,128)(2,1)S(1)} collective-permute-done((bf16[128,1024]{1,0:T(8,128)(2,1)}, bf16[128,1024]{1,0:T(8,128)(2,1)S(1)}, u32[]{:S(2)}, u32[]{:S(2)}) %collective-permute-start.38) | collective-permute-done | bytes 262176 | tf_op jit(solution)/shard_map/ppermute | solution.py:258
  189.3 4.3 %collective-permute-done.34.refs_2_ = bf16[128,1024]{1,0:T(8,128)(2,1)S(1)} collective-permute-done((bf16[128,1024]{1,0:T(8,128)(2,1)S(1)}, bf16[128,1024]{1,0:T(8,128)(2,1)S(1)}, u32[]{:S(2)}, u32[]{:S(2)}) %collective-permute-start.34) | collective-permute-done | bytes 262176 | tf_op jit(solution)/shard_map/ppermute | solution.py:258
  194.4 3.6 %shard_map.99 = (bf16[128,1024]{1,0:T(8,128)(2,1)}, bf16[128,1024]{1,0:T(8,128)(2,1)}) custom-call(s32[1]{0:T(128)} %bitcast.31.place, f32[8,128]{1,0:T(8,128)} %add.78.count, bf16[256,1024]{1,0:T(8,128)(2,1)} %copy-done.11, bf16[256,1024]{1,0:T(8,128)(2,1)} %copy-done.8, bf16[128,1024]{1,0:T(8,128)(2,1)} %copy-done.29, f32[16384,128]{1,0:T(8,128)} %bitcast.67, ...), custom_call_target="tpu_custom_call" | custom-call | flops 2621440 | bytes 2621440 | tf_op jit(solution)/shard_map/pallas_call | solution.py:156
  201.1 7.0 %collective-permute-done.39 = bf16[128,1024]{1,0:T(8,128)(2,1)S(1)} collective-permute-done((bf16[128,1024]{1,0:T(8,128)(2,1)}, bf16[128,1024]{1,0:T(8,128)(2,1)S(1)}, u32[]{:S(2)}, u32[]{:S(2)}) %collective-permute-start.39) | collective-permute-done | bytes 262176 | tf_op jit(solution)/shard_map/ppermute | solution.py:258
  212.5 3.7 %collective-permute-start.43 = (bf16[256,1024]{1,0:T(8,128)(2,1)S(1)}, bf16[256,1024]{1,0:T(8,128)(2,1)S(1)}, u32[]{:S(2)}, u32[]{:S(2)}) collective-permute-start(bf16[256,1024]{1,0:T(8,128)(2,1)S(1)} %pad_maximum_fusion.2), channel_id=1, source_target_pairs={{0,2},{2,0},{4,6},{6,4},{1,3},{3,1},{5,7},{7,5},{8,10},{10,8},{12,... | collective-permute-start | bytes 1572872 | tf_op jit(solution)/shard_map/ppermute | solution.py:258
  216.2 5.8 %fusion.8 = f32[2048,1024]{1,0:T(8,128)} fusion(bf16[1024,2048]{1,0:T(8,128)(2,1)S(1)} %copy-done.3, bf16[256,1024]{1,0:T(8,128)(2,1)S(1)} %pad_maximum_fusion.2, bf16[128,1024]{1,0:T(8,128)(2,1)S(1)} %copy-done.37, bf16[128,1024]{1,0:T(8,128)(2,1)S(1)} %copy-done.39), kind=kOutput, calls=%fused_computation.13 | convolution fusion | flops 2150629376 | bytes 11534336 | tf_op jit(solution)/shard_map/dot_general | solution.py:392
  222.0 7.3 %convolution_add_fusion = f32[2048,1024]{1,0:T(8,128)S(1)} fusion(f32[2048,1024]{1,0:T(8,128)} %fusion.8, bf16[1024,2048]{1,0:T(8,128)(2,1)S(1)} %copy-done.43, bf16[1024,1024]{1,0:T(8,128)(2,1)S(1)} %copy-done.41), kind=kOutput, calls=%fused_computation | convolution fusion | flops 4297064448 | bytes 23068672 | tf_op jit(solution)/shard_map/dot_general | solution.py:392
  240.5 23.2 %shard_map.100 = (f32[16384,128]{1,0:T(8,128)}, f32[16384,128]{1,0:T(8,128)}, f32[16384,128]{1,0:T(8,128)}) custom-call(s32[1]{0:T(128)} %bitcast.place, f32[8,128]{1,0:T(8,128)} %add.78.count, bf16[512,1024]{1,0:T(8,128)(2,1)} %copy-done.6, bf16[512,1024]{1,0:T(8,128)(2,1)} %copy-done.16, bf16[512,1024]{1,0:T(8,128)(2,1)} %copy-done.15, ...), custom_call_target="tpu_custom_call" | custom-call | flops 41943040 | bytes 54525952 | tf_op jit(solution)/shard_map/pallas_call | solution.py:201
  265.3 3.8 %shard_map.101 = bf16[4096,128]{1,0:T(8,128)(2,1)} custom-call(s32[1]{0:T(128)} %bitcast.7.pair, bf16[1024,512]{1,0:T(8,128)(2,1)} %copy-done, bf16[1024,512]{1,0:T(8,128)(2,1)} %copy-done.4, bf16[512,512]{1,0:T(8,128)(2,1)} %copy-done.19, bf16[1024,512]{1,0:T(8,128)(2,1)} %copy-done.1, bf16[1024,512]{1,0:T(8,128)(2,1)} %copy-done.5, bf16[512,512]{1,0:T(8,128)(2,1)} %copy-done.20), custom_call_target="tpu_custom_call" | custom-call | bytes 4194304 | tf_op jit(solution)/shard_map/pallas_call | solution.py:238
  (234 shorter events, 86.8 us)
Async XLA Ops:
  8.8 21.6 %collective-permute-start.8 = (bf16[1024,256]{1,0:T(8,128)(2,1)}, bf16[1024,256]{1,0:T(8,128)(2,1)S(1)}, u32[]{:S(2)}, u32[]{:S(2)}) collective-permute-start(bf16[1024,256]{1,0:T(8,128)(2,1)} %get-tuple-element.66), channel_id=1, source_target_pairs={{0,1},{1,0},{2,3},{3,2},{4,5},{5,4},{6,7},{7,6},{8,9},{9,8},{10,11... | collective-permute-start | bytes 1572872 | tf_op jit(solution)/shard_map/ppermute | solution.py:258
  10.4 20.0 %collective-permute-start.9 = (bf16[1024,256]{1,0:T(8,128)(2,1)}, bf16[1024,256]{1,0:T(8,128)(2,1)S(1)}, u32[]{:S(2)}, u32[]{:S(2)}) collective-permute-start(bf16[1024,256]{1,0:T(8,128)(2,1)} %get-tuple-element.68), channel_id=1, source_target_pairs={{0,16},{8,24},{16,0},{24,8},{1,17},{9,25},{17,1},{25,9},{2,18},{10... | collective-permute-start | bytes 1572872 | tf_op jit(solution)/shard_map/ppermute | solution.py:258
  12.4 22.3 %collective-permute-start.6 = (bf16[1024,256]{1,0:T(8,128)(2,1)}, bf16[1024,256]{1,0:T(8,128)(2,1)S(1)}, u32[]{:S(2)}, u32[]{:S(2)}) collective-permute-start(bf16[1024,256]{1,0:T(8,128)(2,1)} %get-tuple-element.63), channel_id=1, source_target_pairs={{0,24},{8,16},{16,8},{24,0},{1,25},{9,17},{17,9},{25,1},{2,26},{10... | collective-permute-start | bytes 1572872 | tf_op jit(solution)/shard_map/ppermute | solution.py:258
  12.4 22.2 %collective-permute-start.5 = (bf16[1024,256]{1,0:T(8,128)(2,1)S(1)}, bf16[1024,256]{1,0:T(8,128)(2,1)S(1)}, u32[]{:S(2)}, u32[]{:S(2)}) collective-permute-start(bf16[1024,256]{1,0:T(8,128)(2,1)S(1)} %collective-permute-done.4), channel_id=1, source_target_pairs={{0,1},{1,0},{2,3},{3,2},{4,5},{5,4},{6,7},{7,6},{8,9},{9,8},{10,11... | collective-permute-start | bytes 1572872 | tf_op jit(solution)/shard_map/ppermute | solution.py:258
  34.7 25.7 %collective-permute-start.12 = (bf16[512,1024]{1,0:T(8,128)(2,1)S(1)}, bf16[512,1024]{1,0:T(8,128)(2,1)S(1)}, u32[]{:S(2)}, u32[]{:S(2)}) collective-permute-start(bf16[512,1024]{1,0:T(8,128)(2,1)S(1)} %copy-done.17), channel_id=1, source_target_pairs={{0,16},{8,24},{16,0},{24,8},{1,17},{9,25},{17,1},{25,9},{2,18},{10... | collective-permute-start | bytes 3145736 | tf_op jit(solution)/shard_map/ppermute | solution.py:258
  35.4 25.3 %collective-permute-start.11 = (bf16[512,1024]{1,0:T(8,128)(2,1)S(1)}, bf16[512,1024]{1,0:T(8,128)(2,1)S(1)}, u32[]{:S(2)}, u32[]{:S(2)}) collective-permute-start(bf16[512,1024]{1,0:T(8,128)(2,1)S(1)} %copy-done.17), channel_id=1, source_target_pairs={{0,8},{8,0},{16,24},{24,16},{1,9},{9,1},{17,25},{25,17},{2,10},{10... | collective-permute-start | bytes 3145736 | tf_op jit(solution)/shard_map/ppermute | solution.py:258
  36.6 24.1 %collective-permute-start.10 = (bf16[1024,256]{1,0:T(8,128)(2,1)S(1)}, bf16[1024,256]{1,0:T(8,128)(2,1)S(1)}, u32[]{:S(2)}, u32[]{:S(2)}) collective-permute-start(bf16[1024,256]{1,0:T(8,128)(2,1)S(1)} %collective-permute-done.9), channel_id=1, source_target_pairs={{0,1},{1,0},{2,3},{3,2},{4,5},{5,4},{6,7},{7,6},{8,9},{9,8},{10,11... | collective-permute-start | bytes 1572872 | tf_op jit(solution)/shard_map/ppermute | solution.py:258
  38.1 24.2 %collective-permute-start.26 = (bf16[1024,256]{1,0:T(8,128)(2,1)}, bf16[1024,256]{1,0:T(8,128)(2,1)}, u32[]{:S(2)}, u32[]{:S(2)}) collective-permute-start(bf16[1024,256]{1,0:T(8,128)(2,1)} %get-tuple-element.72), channel_id=1, source_target_pairs={{0,8},{8,0},{16,24},{24,16},{1,9},{9,1},{17,25},{25,17},{2,10},{10... | collective-permute-start | bytes 1572872 | tf_op jit(solution)/shard_map/ppermute | solution.py:258
  38.1 24.2 %collective-permute-start.7 = (bf16[1024,256]{1,0:T(8,128)(2,1)S(1)}, bf16[1024,256]{1,0:T(8,128)(2,1)S(1)}, u32[]{:S(2)}, u32[]{:S(2)}) collective-permute-start(bf16[1024,256]{1,0:T(8,128)(2,1)S(1)} %collective-permute-done.6), channel_id=1, source_target_pairs={{0,1},{1,0},{2,3},{3,2},{4,5},{5,4},{6,7},{7,6},{8,9},{9,8},{10,11... | collective-permute-start | bytes 1572872 | tf_op jit(solution)/shard_map/ppermute | solution.py:258
  60.8 14.8 %collective-permute-start.17 = (bf16[1024,256]{1,0:T(8,128)(2,1)S(1)}, bf16[1024,256]{1,0:T(8,128)(2,1)S(1)}, u32[]{:S(2)}, u32[]{:S(2)}) collective-permute-start(bf16[1024,256]{1,0:T(8,128)(2,1)S(1)} %copy-done.21), channel_id=1, source_target_pairs={{0,1},{1,0},{2,3},{3,2},{4,5},{5,4},{6,7},{7,6},{8,9},{9,8},{10,11... | collective-permute-start | bytes 1572872 | tf_op jit(solution)/shard_map/ppermute | solution.py:258
  62.3 27.6 %collective-permute-start.27 = (bf16[1024,256]{1,0:T(8,128)(2,1)}, bf16[1024,256]{1,0:T(8,128)(2,1)}, u32[]{:S(2)}, u32[]{:S(2)}) collective-permute-start(bf16[1024,256]{1,0:T(8,128)(2,1)} %collective-permute-done.26), channel_id=1, source_target_pairs={{0,1},{1,0},{2,3},{3,2},{4,5},{5,4},{6,7},{7,6},{8,9},{9,8},{10,11... | collective-permute-start | bytes 1572872 | tf_op jit(solution)/shard_map/ppermute | solution.py:258
  63.6 23.7 %collective-permute-start.16 = (bf16[1024,256]{1,0:T(8,128)(2,1)}, bf16[1024,256]{1,0:T(8,128)(2,1)}, u32[]{:S(2)}, u32[]{:S(2)}) collective-permute-start(bf16[1024,256]{1,0:T(8,128)(2,1)} %get-tuple-element.77), channel_id=1, source_target_pairs={{0,16},{8,24},{16,0},{24,8},{1,17},{9,25},{17,1},{25,9},{2,18},{10... | collective-permute-start | bytes 1572872 | tf_op jit(solution)/shard_map/ppermute | solution.py:258
  64.4 26.7 %collective-permute-start.24 = (bf16[1024,256]{1,0:T(8,128)(2,1)}, bf16[1024,256]{1,0:T(8,128)(2,1)}, u32[]{:S(2)}, u32[]{:S(2)}) collective-permute-start(bf16[1024,256]{1,0:T(8,128)(2,1)} %get-tuple-element.88), channel_id=1, source_target_pairs={{0,24},{8,16},{16,8},{24,0},{1,25},{9,17},{17,9},{25,1},{2,26},{10... | collective-permute-start | bytes 1572872 | tf_op jit(solution)/shard_map/ppermute | solution.py:258
  66.1 15.6 %collective-permute-start.14 = (bf16[256,1024]{1,0:T(8,128)(2,1)S(1)}, bf16[256,1024]{1,0:T(8,128)(2,1)S(1)}, u32[]{:S(2)}, u32[]{:S(2)}) collective-permute-start(bf16[256,1024]{1,0:T(8,128)(2,1)S(1)} %convolution_convert_fusion.7), channel_id=1, source_target_pairs={{0,2},{6,4},{1,3},{7,5},{8,10},{14,12},{9,11},{15,13},{16,18},{22,... | collective-permute-start | bytes 1572872 | tf_op jit(solution)/shard_map/ppermute | solution.py:278
  82.0 16.2 %collective-permute-start.23 = (bf16[256,1024]{1,0:T(8,128)(2,1)S(1)}, bf16[256,1024]{1,0:T(8,128)(2,1)S(1)}, u32[]{:S(2)}, u32[]{:S(2)}) collective-permute-start(bf16[256,1024]{1,0:T(8,128)(2,1)S(1)} %convolution_convert_fusion.5), channel_id=1, source_target_pairs={{0,2},{6,4},{1,3},{7,5},{8,10},{14,12},{9,11},{15,13},{16,18},{22,... | collective-permute-start | bytes 1572872 | tf_op jit(solution)/shard_map/ppermute | solution.py:278
  86.4 15.1 %collective-permute-start.15 = (bf16[256,1024]{1,0:T(8,128)(2,1)S(1)}, bf16[256,1024]{1,0:T(8,128)(2,1)S(1)}, u32[]{:S(2)}, u32[]{:S(2)}) collective-permute-start(bf16[256,1024]{1,0:T(8,128)(2,1)S(1)} %add_convert_fusion.4), channel_id=1, source_target_pairs={{2,4},{4,2},{3,5},{5,3},{10,12},{12,10},{11,13},{13,11},{18,20},{2... | collective-permute-start | bytes 1572872 | tf_op jit(solution)/shard_map/ppermute | solution.py:282
  99.1 19.3 %collective-permute-start.25 = (bf16[256,1024]{1,0:T(8,128)(2,1)}, bf16[256,1024]{1,0:T(8,128)(2,1)S(1)}, u32[]{:S(2)}, u32[]{:S(2)}) collective-permute-start(bf16[256,1024]{1,0:T(8,128)(2,1)} %add_convert_fusion.3), channel_id=1, source_target_pairs={{2,4},{4,2},{3,5},{5,3},{10,12},{12,10},{11,13},{13,11},{18,20},{2... | collective-permute-start | bytes 1572872 | tf_op jit(solution)/shard_map/ppermute | solution.py:282
  99.8 18.6 %collective-permute-start.28 = (bf16[1024,256]{1,0:T(8,128)(2,1)}, bf16[1024,256]{1,0:T(8,128)(2,1)S(1)}, u32[]{:S(2)}, u32[]{:S(2)}) collective-permute-start(bf16[1024,256]{1,0:T(8,128)(2,1)} %collective-permute-done.24), channel_id=1, source_target_pairs={{0,1},{1,0},{2,3},{3,2},{4,5},{5,4},{6,7},{7,6},{8,9},{9,8},{10,11... | collective-permute-start | bytes 1572872 | tf_op jit(solution)/shard_map/ppermute | solution.py:258
  118.5 35.1 %collective-permute-start.29 = (bf16[128,1024]{1,0:T(8,128)(2,1)S(1)}, bf16[128,1024]{1,0:T(8,128)(2,1)S(1)}, u32[]{:S(2)}, u32[]{:S(2)}) collective-permute-start(bf16[128,1024]{1,0:T(8,128)(2,1)S(1)} %add_convert_fusion.7), channel_id=1, source_target_pairs={{0,2},{2,0},{4,6},{6,4},{1,3},{3,1},{5,7},{7,5},{8,10},{10,8},{12,... | collective-permute-start | bytes 786440 | tf_op jit(solution)/shard_map/ppermute | solution.py:258
  128.2 15.9 %collective-permute-start.31 = (bf16[256,1024]{1,0:T(8,128)(2,1)S(1)}, bf16[256,1024]{1,0:T(8,128)(2,1)S(1)}, u32[]{:S(2)}, u32[]{:S(2)}) collective-permute-start(bf16[256,1024]{1,0:T(8,128)(2,1)S(1)} %convolution_convert_fusion.3), channel_id=1, source_target_pairs={{0,2},{6,4},{1,3},{7,5},{8,10},{14,12},{9,11},{15,13},{16,18},{22,... | collective-permute-start | bytes 1572872 | tf_op jit(solution)/shard_map/ppermute | solution.py:278
  134.4 18.3 %collective-permute-start.22 = (bf16[256,1024]{1,0:T(8,128)(2,1)S(1)}, bf16[256,1024]{1,0:T(8,128)(2,1)S(1)}, u32[]{:S(2)}, u32[]{:S(2)}) collective-permute-start(bf16[256,1024]{1,0:T(8,128)(2,1)S(1)} %collective-permute-done.21), channel_id=1, source_target_pairs={{2,0},{4,6},{3,1},{5,7},{10,8},{12,14},{11,9},{13,15},{18,16},{20,... | collective-permute-start | bytes 1572872 | tf_op jit(solution)/shard_map/ppermute | solution.py:289
  137.8 24.0 %collective-permute-start.30 = (bf16[256,1024]{1,0:T(8,128)(2,1)}, bf16[256,1024]{1,0:T(8,128)(2,1)S(1)}, u32[]{:S(2)}, u32[]{:S(2)}) collective-permute-start(bf16[256,1024]{1,0:T(8,128)(2,1)} %convolution_convert_fusion.1), channel_id=1, source_target_pairs={{0,2},{2,0},{4,6},{6,4},{1,3},{3,1},{5,7},{7,5},{8,10},{10,8},{12,... | collective-permute-start | bytes 1572872 | tf_op jit(solution)/shard_map/ppermute | solution.py:258
  144.3 17.5 %collective-permute-start.32 = (bf16[256,1024]{1,0:T(8,128)(2,1)S(1)}, bf16[256,1024]{1,0:T(8,128)(2,1)S(1)}, u32[]{:S(2)}, u32[]{:S(2)}) collective-permute-start(bf16[256,1024]{1,0:T(8,128)(2,1)S(1)} %add_convert_fusion.2), channel_id=1, source_target_pairs={{2,4},{4,2},{3,5},{5,3},{10,12},{12,10},{11,13},{13,11},{18,20},{2... | collective-permute-start | bytes 1572872 | tf_op jit(solution)/shard_map/ppermute | solution.py:282
  164.7 22.6 %collective-permute-start.36 = (bf16[256,1024]{1,0:T(8,128)(2,1)S(1)}, bf16[256,1024]{1,0:T(8,128)(2,1)}, u32[]{:S(2)}, u32[]{:S(2)}) collective-permute-start(bf16[256,1024]{1,0:T(8,128)(2,1)S(1)} %pad_maximum_fusion.1), channel_id=1, source_target_pairs={{2,4},{4,2},{3,5},{5,3},{10,12},{12,10},{11,13},{13,11},{18,20},{2... | collective-permute-start | bytes 1572872 | tf_op jit(solution)/shard_map/ppermute | solution.py:288
  177.8 15.8 %collective-permute-start.34 = (bf16[128,1024]{1,0:T(8,128)(2,1)S(1)}, bf16[128,1024]{1,0:T(8,128)(2,1)S(1)}, u32[]{:S(2)}, u32[]{:S(2)}) collective-permute-start(bf16[128,1024]{1,0:T(8,128)(2,1)S(1)} %add_convert_fusion.6), channel_id=1, source_target_pairs={{0,4},{2,6},{4,0},{6,2},{1,5},{3,7},{5,1},{7,3},{8,12},{10,14},{12... | collective-permute-start | bytes 786440 | tf_op jit(solution)/shard_map/ppermute | solution.py:258
  186.6 22.5 %collective-permute-start.41 = (bf16[256,1024]{1,0:T(8,128)(2,1)S(1)}, bf16[256,1024]{1,0:T(8,128)(2,1)S(1)}, u32[]{:S(2)}, u32[]{:S(2)}) collective-permute-start(bf16[256,1024]{1,0:T(8,128)(2,1)S(1)} %pad_maximum_fusion.3), channel_id=1, source_target_pairs={{2,4},{4,2},{3,5},{5,3},{10,12},{12,10},{11,13},{13,11},{18,20},{2... | collective-permute-start | bytes 1572872 | tf_op jit(solution)/shard_map/ppermute | solution.py:288
  187.3 23.3 %collective-permute-start.37 = (bf16[256,1024]{1,0:T(8,128)(2,1)}, bf16[256,1024]{1,0:T(8,128)(2,1)S(1)}, u32[]{:S(2)}, u32[]{:S(2)}) collective-permute-start(bf16[256,1024]{1,0:T(8,128)(2,1)} %collective-permute-done.36), channel_id=1, source_target_pairs={{2,0},{4,6},{3,1},{5,7},{10,8},{12,14},{11,9},{13,15},{18,16},{20,... | collective-permute-start | bytes 1572872 | tf_op jit(solution)/shard_map/ppermute | solution.py:289
  199.2 30.1 %collective-permute-start.40 = (bf16[512,1024]{1,0:T(8,128)(2,1)S(1)}, bf16[512,1024]{1,0:T(8,128)(2,1)S(1)}, u32[]{:S(2)}, u32[]{:S(2)}) collective-permute-start(bf16[512,1024]{1,0:T(8,128)(2,1)S(1)} %constant_dynamic-update-slice_fusion.20.refs_0_), channel_id=1, source_target_pairs={{0,16},{8,24},{16,0},{24,8},{1,17},{9,25},{17,1},{25,9},{2,18},{10... | collective-permute-start | bytes 3145736 | tf_op jit(solution)/shard_map/ppermute | solution.py:258
  209.1 20.2 %collective-permute-start.42 = (bf16[256,1024]{1,0:T(8,128)(2,1)S(1)}, bf16[256,1024]{1,0:T(8,128)(2,1)S(1)}, u32[]{:S(2)}, u32[]{:S(2)}) collective-permute-start(bf16[256,1024]{1,0:T(8,128)(2,1)S(1)} %collective-permute-done.41), channel_id=1, source_target_pairs={{2,0},{4,6},{3,1},{5,7},{10,8},{12,14},{11,9},{13,15},{18,16},{20,... | collective-permute-start | bytes 1572872 | tf_op jit(solution)/shard_map/ppermute | solution.py:289
  212.5 18.0 %collective-permute-start.43 = (bf16[256,1024]{1,0:T(8,128)(2,1)S(1)}, bf16[256,1024]{1,0:T(8,128)(2,1)S(1)}, u32[]{:S(2)}, u32[]{:S(2)}) collective-permute-start(bf16[256,1024]{1,0:T(8,128)(2,1)S(1)} %pad_maximum_fusion.2), channel_id=1, source_target_pairs={{0,2},{2,0},{4,6},{6,4},{1,3},{3,1},{5,7},{7,5},{8,10},{10,8},{12,... | collective-permute-start | bytes 1572872 | tf_op jit(solution)/shard_map/ppermute | solution.py:258
  235.8 27.8 %collective-permute-start.48 = (bf16[512,512]{1,0:T(8,128)(2,1)S(1)}, bf16[512,512]{1,0:T(8,128)(2,1)S(1)}, u32[]{:S(2)}, u32[]{:S(2)}) collective-permute-start(bf16[512,512]{1,0:T(8,128)(2,1)S(1)} %add_convert_fusion), channel_id=1, source_target_pairs={{0,16},{8,24},{16,0},{24,8},{1,17},{9,25},{17,1},{25,9},{2,18},{10... | collective-permute-start | bytes 1572872 | tf_op jit(solution)/shard_map/ppermute | solution.py:258
  238.8 24.9 %collective-permute-start.49 = (bf16[512,512]{1,0:T(8,128)(2,1)}, bf16[512,512]{1,0:T(8,128)(2,1)S(1)}, u32[]{:S(2)}, u32[]{:S(2)}) collective-permute-start(bf16[512,512]{1,0:T(8,128)(2,1)} %add_convert_fusion.1), channel_id=1, source_target_pairs={{0,16},{8,24},{16,0},{24,8},{1,17},{9,25},{17,1},{25,9},{2,18},{10... | collective-permute-start | bytes 1572872 | tf_op jit(solution)/shard_map/ppermute | solution.py:258
  (62 other events, 681.8 us)
